TPU v7x, 256 devices: a whole 4x4x8 slice. The times are simulated.
256 devices in a mesh: seq: 32 (over z, y_lo, core), tp: 8 (over y_hi, x).
Axes of the slice: x: 4, y: 4 (y_hi: 2, y_lo: 2; y = y_hi * 2 + y_lo), z: 8, core: 2. Of those that a mesh axis runs over, the one named last changes fastest.
Arguments:
- queries: bfloat16 [16384, 8192], P('seq', 'tp'), may hold values from -6 to 6
- key_inputs: bfloat16 [16384, 8192], P('seq', 'tp'), may hold values from -6 to 6
- value_inputs: bfloat16 [16384, 8192], P('seq', 'tp'), may hold values from -6 to 6
- filters: bfloat16 [512, 128], P('tp'), may hold values from -0.5 to 0.5
- doc_ids: int32 [16384], P('seq'), may hold values from 0 to 31, never falling along the last dimension, each value on 1 to 1024 neighbouring positions
- cotangent: bfloat16 [16384, 8192], P('seq', 'tp'), may hold values from -200 to 200
Outputs:
- gated_out: bfloat16 [16384, 8192], P('seq', 'tp')
- grad_queries: bfloat16 [16384, 8192], P('seq', 'tp')
- grad_keys: bfloat16 [16384, 8192], P('seq', 'tp')
- grad_values: bfloat16 [16384, 8192], P('seq', 'tp')
- grad_filters: float32 [512, 128], P('tp')
Inputs may be any that keep to these rules, and one draw needn't show every extreme that they name: `doc_ids`: documents are runs of consecutive positions numbered 0, 1, 2, ... in order of position; each has 1 to 1024 positions, and one has exactly 1024.
All inputs are finite; a program needn't handle non-finite values.
Results may differ from a plain program's by a relative error of at most 0.0053.
Values may be sent and summed in bfloat16 or wider, within the bound.
A program may use at most 64 MiB of HBM per device.

v0:
```python
import math

import jax
import jax.numpy as jnp
from jax import lax
from jax.sharding import PartitionSpec as P


def with_halo(cells, sides, width):
    for axis, dim in sides:
        count = lax.axis_size(axis)
        ends = count - 1
        head = lax.slice_in_dim(cells, 0, width, axis=dim)
        tail = lax.slice_in_dim(cells, cells.shape[dim] - width, cells.shape[dim], axis=dim)
        cells = jnp.concatenate(
            [
                lax.ppermute(tail, axis, [(i, (i + 1) % count) for i in range(ends)]),
                cells,
                lax.ppermute(head, axis, [((i + 1) % count, i) for i in range(ends)]),
            ],
            axis=dim,
        )
    return cells


def from_behind(value, axis, steps):
    count = lax.axis_size(axis)
    leading, last = (max(0, -steps), min(count, count - steps))
    return lax.ppermute(value, axis, [(source, source + steps) for source in range(leading, last)])


def to_lanes(rows_major, tap_count, groups):
    row_count, chan_count = rows_major.shape
    blocks = row_count // tap_count
    turned = rows_major.reshape(blocks, tap_count, chan_count).transpose(0, 2, 1)
    return turned.reshape(blocks, groups, chan_count // groups, tap_count)


def from_lanes(lanes):
    blocks, groups, group_size, tap_count = lanes.shape
    turned = lanes.reshape(blocks, groups * group_size, tap_count).transpose(0, 2, 1)
    return turned.reshape(blocks * tap_count, groups * group_size)


def local(queries, key_inputs, value_inputs, filters, doc_ids, cotangent):
    row_count, chan_count = queries.shape
    groups, tap_count = filters.shape
    blocks = row_count // tap_count
    rim_rows = tap_count - 1
    doc_halo = with_halo(doc_ids, (("seq", 0),), rim_rows)
    left_docs = doc_halo[:rim_rows]
    right_docs = doc_halo[rim_rows + row_count :]
    own_docs = doc_ids.reshape(blocks, tap_count)
    prev_docs = jnp.concatenate(
        [left_docs[:1], left_docs, doc_ids[: row_count - tap_count]]
    ).reshape(blocks, tap_count)
    next_docs = jnp.concatenate([doc_ids[tap_count:], right_docs, right_docs[-1:]]).reshape(
        blocks, tap_count
    )
    same_cur = (own_docs[:, :, None] == own_docs[:, None, :]).astype(jnp.bfloat16)
    same_prev = (prev_docs[:, :, None] == own_docs[:, None, :]).astype(jnp.bfloat16)
    same_next = (own_docs[:, :, None] == next_docs[:, None, :]).astype(jnp.bfloat16)
    product = (key_inputs.astype(jnp.float32) * value_inputs.astype(jnp.float32)).astype(
        jnp.bfloat16
    )
    key_rim, value_rim = from_behind(
        (key_inputs[row_count - rim_rows :], value_inputs[row_count - rim_rows :]), "seq", 1
    )
    product_rim = (key_rim.astype(jnp.float32) * value_rim.astype(jnp.float32)).astype(jnp.bfloat16)
    grad_z = (cotangent.astype(jnp.float32) * queries.astype(jnp.float32)).astype(jnp.bfloat16)
    grad_rim = from_behind(grad_z[:rim_rows], "seq", -1)
    zero_row = jnp.zeros((1, chan_count), jnp.bfloat16)
    prod_lanes = to_lanes(product, tap_count, groups)
    grad_lanes = to_lanes(grad_z, tap_count, groups)
    prod_before = jnp.concatenate(
        [
            to_lanes(jnp.concatenate([zero_row, product_rim], axis=0), tap_count, groups),
            prod_lanes[:-1],
        ],
        axis=0,
    )
    grad_after = jnp.concatenate(
        [
            grad_lanes[1:],
            to_lanes(jnp.concatenate([grad_rim, zero_row], axis=0), tap_count, groups),
        ],
        axis=0,
    )
    lag_index = jnp.arange(tap_count, dtype=jnp.int32)
    window_pos = jnp.arange(2 * tap_count, dtype=jnp.int32)
    band_lag = (lag_index[None, :] - window_pos[:, None] + tap_count).reshape(
        1, 2 * tap_count * tap_count
    )
    lag_table = (band_lag == lag_index[:, None]).astype(jnp.bfloat16)
    band = jnp.dot(filters, lag_table, preferred_element_type=jnp.float32).astype(jnp.bfloat16)
    band = band.reshape(groups, 2 * tap_count, tap_count)
    upper_band = band[:, :tap_count]
    lower_band = band[:, tap_count:]
    mat_cur = lower_band[None] * same_cur[:, None]
    mat_prev = upper_band[None] * same_prev[:, None]
    mat_next = upper_band[None] * same_next[:, None]
    conv_lanes = jnp.einsum(
        "bgcs,bgsi->bgci", prod_lanes, mat_cur, preferred_element_type=jnp.float32
    )
    conv_lanes = conv_lanes + jnp.einsum(
        "bgcs,bgsi->bgci", prod_before, mat_prev, preferred_element_type=jnp.float32
    )
    back_lanes = jnp.einsum(
        "bgcs,bgis->bgci", grad_lanes, mat_cur, preferred_element_type=jnp.float32
    )
    back_lanes = back_lanes + jnp.einsum(
        "bgcs,bgis->bgci", grad_after, mat_next, preferred_element_type=jnp.float32
    )
    pair_cur = jnp.sum(
        jnp.einsum("bgcs,bgci->bgsi", prod_lanes, grad_lanes, preferred_element_type=jnp.float32)
        * same_cur[:, None],
        axis=0,
    )
    pair_prev = jnp.sum(
        jnp.einsum("bgcs,bgci->bgsi", prod_before, grad_lanes, preferred_element_type=jnp.float32)
        * same_prev[:, None],
        axis=0,
    )
    below = lag_index[:, None] <= lag_index[None, :]
    merged = jnp.where(below[None], pair_cur, pair_prev).reshape(groups, tap_count * tap_count)
    pair_lag = ((lag_index[None, :] - lag_index[:, None] + tap_count) % tap_count).reshape(
        tap_count * tap_count, 1
    )
    diag_table = (pair_lag == lag_index[None, :]).astype(jnp.float32)
    filter_raw = jnp.dot(
        merged, diag_table, precision=lax.Precision.HIGHEST, preferred_element_type=jnp.float32
    )
    conv_full = from_lanes(conv_lanes)
    grad_product = from_lanes(back_lanes)
    gated_out = (queries.astype(jnp.float32) * conv_full).astype(jnp.bfloat16)
    grad_queries = (cotangent.astype(jnp.float32) * conv_full).astype(jnp.bfloat16)
    grad_keys = (grad_product * value_inputs.astype(jnp.float32)).astype(jnp.bfloat16)
    grad_values = (grad_product * key_inputs.astype(jnp.float32)).astype(jnp.bfloat16)
    group_size = chan_count // groups
    clip_bound = 1.5 * math.sqrt(
        groups * lax.axis_size("tp") * tap_count * group_size * row_count * lax.axis_size("seq")
    )
    summed = lax.psum(filter_raw, "seq")
    energy = lax.psum(jnp.sum(summed * summed), "tp")
    factor = jnp.minimum(1.0, clip_bound / (jnp.sqrt(energy) + 1e-06))
    grad_filters = summed * factor
    return (gated_out, grad_queries, grad_keys, grad_values, grad_filters)


def solution(mesh):
    in_specs = (
        P("seq", "tp"),
        P("seq", "tp"),
        P("seq", "tp"),
        P("tp", None),
        P("seq"),
        P("seq", "tp"),
    )
    out_specs = (P("seq", "tp"), P("seq", "tp"), P("seq", "tp"), P("seq", "tp"), P("tp", None))
    return jax.shard_map(local, mesh=mesh, in_specs=in_specs, out_specs=out_specs, check_vma=False)
```

profile of v0, /device:TPU:128, one launch (start us, length us, event | category | flops | bytes accessed | tf_op | source)
XLA Modules:
  0.0 220.5 jit_solution(14894283781308637797)
XLA Ops:
  1.5 1.9 collective-permute-start.2
  3.4 5.8 %collective-permute-start.4 = (s32[127]{0:T(128)S(1)}, s32[127]{0:T(128)S(1)}, u32[]{:S(2)}, u32[]{:S(2)}) collective-permute-start(s32[127]{0:T(128)S(1)} %get-tuple-element.19), channel_id=1, source_target_pairs={{8,0},{16,8},{24,16},{32,24},{40,32},{48,40},{56,48},{64,56},{72,6... | collective-permute-start | bytes 1532 | tf_op jit(solution)/shard_map/ppermute | solution.py:19
  9.2 1.9 fusion.28
  11.1 1.9 collective-permute-start.3
  13.1 1.7 slice.47
  14.8 2.4 %collective-permute-start.1 = (bf16[127,1024]{1,0:T(8,128)(2,1)}, bf16[127,1024]{1,0:T(8,128)(2,1)S(1)}, u32[]{:S(2)}, u32[]{:S(2)}) collective-permute-start(bf16[127,1024]{1,0:T(8,128)(2,1)} %slice.47), channel_id=1, source_target_pairs={{0,8},{8,16},{16,24},{24,32},{32,40},{40,48},{48,56},{56,64},{64,7... | collective-permute-start | bytes 780296 | tf_op jit(solution)/shard_map/ppermute | solution.py:29
  17.2 1.7 slice.46
  18.9 1.9 collective-permute-start
  20.9 3.9 %fusion.22 = bf16[8,8,256,128]{3,1,2,0:T(8,128)(2,1)S(1)} fusion(bf16[64,128]{1,0:T(8,128)(2,1)S(1)} %copy-done, s32[32768]{0:T(1024)S(1)} %add_bitcast_fusion), kind=kOutput, calls=%fused_computation.34 | convolution fusion | flops 543162368 | bytes 4341760 | tf_op jit(solution)/shard_map/dot_general | solution.py:95
  24.8 1.2 copy.17
  26.0 2.3 %fusion.46 = (bf16[64,128,128]{2,1,0:T(8,128)(2,1)}, bf16[64,128,128]{2,1,0:T(8,128)(2,1)}) fusion(bf16[64,256,128]{2,1,0:T(8,128)(2,1)S(1)} %bitcast.66), kind=kLoop, calls=%fused_computation.70 | loop fusion | bytes 8388608 | tf_op jit(solution)/shard_map/slice | solution.py:97
  31.6 7.4 %fusion = f32[4,64,16,128]{3,2,1,0:T(8,128)} fusion(bf16[4,64,16,128]{3,2,1,0:T(8,128)(2,1)S(1)} %bitcast.72, bf16[4,128,128]{2,1,0:T(8,128)(2,1)S(1)} %get-tuple-element.15, bf16[64,128,128]{2,1,0:T(8,128)(2,1)} %get-tuple-element.6), kind=kOutput, calls=%fused_computation.4 | convolution fusion | flops 138412032 | bytes 5373952 | tf_op jit(solution)/shard_map/bgcs,bgis->bgci/dot_general | solution.py:108
  39.2 7.1 %fusion.33 = f32[4,64,16,128]{3,2,1,0:T(8,128)} fusion(f32[4,64,16,128]{3,2,1,0:T(8,128)} %fusion, bf16[4,128,128]{2,1,0:T(8,128)(2,1)S(1)} %get-tuple-element.16, bf16[64,128,128]{2,1,0:T(8,128)(2,1)} %get-tuple-element.5, bf16[1,64,16,128]{3,2,1,0:T(8,128)(2,1)S(1)} %bitcast.85, bf16[3,64,16,128]{3,2,1,0:T(8,128)(2,1)S(1)} %bitcast.80), kind=kOutput, calls=%fused_computation.43 | convolution fusion | flops 139460608 | bytes 7471104 | tf_op jit(solution)/shard_map/bgcs,bgis->bgci/dot_general | solution.py:111
  46.3 1.9 copy.16
  48.3 3.8 %fusion.24 = (bf16[512,1024]{1,0:T(8,128)(2,1)}, bf16[512,1024]{1,0:T(8,128)(2,1)}, bf16[512,1024]{1,0:T(8,128)(2,1)S(1)}) fusion(bf16[512,1024]{1,0:T(8,128)(2,1)} %param.7, f32[4,128,1024]{2,1,0:T(8,128)S(1)} %copy.16, bf16[512,1024]{1,0:T(8,128)(2,1)} %param.8), kind=kLoop, calls=%fused_computation.36 | loop fusion | flops 4194304 | bytes 7340032 | tf_op jit(solution)/shard_map/convert_element_type | solution.py:138
  52.8 5.9 %fusion.2 = f32[4,64,16,128]{3,2,1,0:T(8,128)} fusion(bf16[4,64,16,128]{3,2,1,0:T(8,128)(2,1)S(1)} %bitcast.76, bf16[4,128,128]{2,1,0:T(8,128)(2,1)} %copy-done.11, bf16[64,128,128]{2,1,0:T(8,128)(2,1)} %get-tuple-element.6), kind=kOutput, calls=%fused_computation.6 | convolution fusion | flops 138412032 | bytes 5373952 | tf_op jit(solution)/shard_map/bgcs,bgsi->bgci/dot_general | solution.py:102
  60.0 5.0 %fusion.30 = f32[4,64,16,128]{3,2,1,0:T(8,128)} fusion(f32[4,64,16,128]{3,2,1,0:T(8,128)} %fusion.2, bf16[4,128,128]{2,1,0:T(8,128)(2,1)S(1)} %copy-done.10, bf16[64,128,128]{2,1,0:T(8,128)(2,1)} %get-tuple-element.5, bf16[3,64,16,128]{3,2,1,0:T(8,128)(2,1)S(1)} %bitcast.81, bf16[1,64,16,128]{3,2,1,0:T(8,128)(2,1)S(1)} %bitcast.83), kind=kOutput, calls=%fused_computation.42 | convolution fusion | flops 139460608 | bytes 7471104 | tf_op jit(solution)/shard_map/bgcs,bgsi->bgci/dot_general | solution.py:105
  65.0 2.2 %copy.13 = f32[4,128,1024]{2,1,0:T(8,128)S(1)} copy(f32[4,128,1024]{1,2,0:T(8,128)} %bitcast.79) | data formatting | bytes 4194304 | tf_op jit(solution)/shard_map/transpose | solution.py:41
  67.3 4.3 %multiply_reduce_fusion = f32[64,128,128]{2,1,0:T(8,128)S(1)} fusion(bf16[4,64,16,128]{3,2,1,0:T(8,128)(2,1)S(1)} %bitcast.73, f32[4,128,128]{2,1,0:T(8,128)S(1)} %copy-done.8, bf16[3,64,16,128]{3,2,1,0:T(8,128)(2,1)} %bitcast.82, bf16[1,64,16,128]{3,2,1,0:T(8,128)(2,1)} %bitcast.84), kind=kOutput, calls=%fused_computation.1 | convolution fusion | flops 142082048 | bytes 6553600 | tf_op jit(solution)/shard_map/bgcs,bgci->bgsi/dot_general | solution.py:120
  71.6 3.1 %multiply_reduce_fusion.1 = f32[64,128,128]{2,1,0:T(8,128)S(1)} fusion(bf16[4,64,16,128]{3,2,1,0:T(8,128)(2,1)S(1)} %bitcast.77, bf16[4,64,16,128]{3,2,1,0:T(8,128)(2,1)S(1)} %bitcast.74, f32[4,128,128]{2,1,0:T(8,128)S(1)} %copy-done.7), kind=kOutput, calls=%fused_computation.2 | convolution fusion | flops 141557760 | bytes 6553600 | tf_op jit(solution)/shard_map/bgcs,bgci->bgsi/dot_general | solution.py:115
  74.7 7.3 %fusion.9 = f32[64,128]{1,0:T(8,128)S(1)} fusion(f32[8,8,128,128]{3,2,1,0:T(8,128)S(1)} %bitcast.69, f32[8,8,128,128]{3,2,1,0:T(8,128)S(1)} %bitcast.70, s32[16384]{0:T(1024)S(1)} %add_select_fusion, pred[16384]{0:T(1024)(128)(4,1)S(1)} %fusion.40), kind=kOutput, calls=%fused_computation.14 | convolution fusion | flops 1613758464 | bytes 8503296 | tf_op jit(solution)/shard_map/dot_general | solution.py:130
  82.0 108.3 %psum.14 = f32[64,128]{1,0:T(8,128)S(1)} all-reduce(f32[64,128]{1,0:T(8,128)S(1)} %fusion.9), channel_id=1, replica_groups=mesh['seq'=32,'tp'=8] {'seq'}, use_global_device_ids=true, to_apply=%region_2.3 | all-reduce | flops 8192 | bytes 65536 | tf_op jit(solution)/shard_map/psum | solution.py:143
  190.9 3.3 %fusion.27 = (bf16[512,1024]{1,0:T(8,128)(2,1)}, bf16[512,1024]{1,0:T(8,128)(2,1)}) fusion(bf16[512,1024]{1,0:T(8,128)(2,1)S(1)} %copy-done.1, f32[4,128,1024]{2,1,0:T(8,128)S(1)} %copy.13, bf16[512,1024]{1,0:T(8,128)(2,1)} %param.6), kind=kLoop, calls=%fused_computation.39 | loop fusion | flops 3145728 | bytes 6291456 | tf_op jit(solution)/shard_map/convert_element_type | solution.py:136
  194.2 25.0 %psum.15 = f32[]{:T(128)} all-reduce(f32[]{:T(128)} %multiply_reduce_fusion.2), channel_id=1, replica_groups=mesh['seq'=32,'tp'=8] {'tp'}, use_global_device_ids=true, to_apply=%region_4.5 | all-reduce | flops 1 | bytes 8 | tf_op jit(solution)/shard_map/psum | solution.py:144
  (52 shorter events, 7.7 us)
Async XLA Ops:
  0.6 20.3 %copy-start = (bf16[64,128]{1,0:T(8,128)(2,1)S(1)}, bf16[64,128]{1,0:T(8,128)(2,1)}, u32[]{:S(2)}) copy-start(bf16[64,128]{1,0:T(8,128)(2,1)} %param.9) | copy-start | bytes 49156
  1.5 28.2 %collective-permute-start.2 = (s32[127]{0:T(128)S(1)}, s32[127]{0:T(128)S(1)}, u32[]{:S(2)}, u32[]{:S(2)}) collective-permute-start(s32[127]{0:T(128)S(1)} %get-tuple-element.20), channel_id=1, source_target_pairs={{0,8},{8,16},{16,24},{24,32},{32,40},{40,48},{48,56},{56,64},{64,7... | collective-permute-start | bytes 1532 | tf_op jit(solution)/shard_map/ppermute | solution.py:17
  3.4 25.6 %collective-permute-start.4 = (s32[127]{0:T(128)S(1)}, s32[127]{0:T(128)S(1)}, u32[]{:S(2)}, u32[]{:S(2)}) collective-permute-start(s32[127]{0:T(128)S(1)} %get-tuple-element.19), channel_id=1, source_target_pairs={{8,0},{16,8},{24,16},{32,24},{40,32},{48,40},{56,48},{64,56},{72,6... | collective-permute-start | bytes 1532 | tf_op jit(solution)/shard_map/ppermute | solution.py:19
  11.1 27.9 %collective-permute-start.3 = (bf16[127,1024]{1,0:T(8,128)(2,1)S(1)}, bf16[127,1024]{1,0:T(8,128)(2,1)S(1)}, u32[]{:S(2)}, u32[]{:S(2)}) collective-permute-start(bf16[127,1024]{1,0:T(8,128)(2,1)S(1)} %slice.64), channel_id=1, source_target_pairs={{8,0},{16,8},{24,16},{32,24},{40,32},{48,40},{56,48},{64,56},{72,6... | collective-permute-start | bytes 780296 | tf_op jit(solution)/shard_map/ppermute | solution.py:29
  14.8 43.9 %collective-permute-start.1 = (bf16[127,1024]{1,0:T(8,128)(2,1)}, bf16[127,1024]{1,0:T(8,128)(2,1)S(1)}, u32[]{:S(2)}, u32[]{:S(2)}) collective-permute-start(bf16[127,1024]{1,0:T(8,128)(2,1)} %slice.47), channel_id=1, source_target_pairs={{0,8},{8,16},{16,24},{24,32},{32,40},{40,48},{48,56},{56,64},{64,7... | collective-permute-start | bytes 780296 | tf_op jit(solution)/shard_map/ppermute | solution.py:29
  18.9 39.8 %collective-permute-start = (bf16[127,1024]{1,0:T(8,128)(2,1)}, bf16[127,1024]{1,0:T(8,128)(2,1)}, u32[]{:S(2)}, u32[]{:S(2)}) collective-permute-start(bf16[127,1024]{1,0:T(8,128)(2,1)} %slice.46), channel_id=1, source_target_pairs={{0,8},{8,16},{16,24},{24,32},{32,40},{40,48},{48,56},{56,64},{64,7... | collective-permute-start | bytes 780296 | tf_op jit(solution)/shard_map/ppermute | solution.py:29
  25.9 2.3 %copy-start.12 = (s32[512]{0:T(512)S(1)}, s32[512]{0:T(512)}, u32[]{:S(2)}) copy-start(s32[512]{0:T(512)} %param.10) | copy-start | bytes 6148
  28.9 10.1 %copy-start.2 = (bf16[4,128,1024]{1,2,0:T(8,128)(2,1)}, bf16[4,128,1024]{1,2,0:T(8,128)(2,1)S(1)}, u32[]{:S(2)}) copy-start(bf16[4,128,1024]{1,2,0:T(8,128)(2,1)S(1)} %copy.14) | copy-start | bytes 3145732
  31.6 7.5 %copy-start.11 = (bf16[4,128,128]{2,1,0:T(8,128)(2,1)}, bf16[4,128,128]{2,1,0:T(8,128)(2,1)S(1)}, u32[]{:S(2)}) copy-start(bf16[4,128,128]{2,1,0:T(8,128)(2,1)S(1)} %get-tuple-element.15) | copy-start | bytes 393220
  52.7 6.0 %copy-start.4 = (bf16[4,128,1024]{1,2,0:T(8,128)(2,1)}, bf16[4,128,1024]{1,2,0:T(8,128)(2,1)S(1)}, u32[]{:S(2)}) copy-start(bf16[4,128,1024]{1,2,0:T(8,128)(2,1)S(1)} %copy.11) | copy-start | bytes 3145732
  52.8 7.2 %copy-start.6 = (bf16[3,1024,128]{2,1,0:T(8,128)(2,1)}, bf16[3,1024,128]{2,1,0:T(8,128)(2,1)S(1)}, u32[]{:S(2)}) copy-start(bf16[3,1024,128]{2,1,0:T(8,128)(2,1)S(1)} %slice.61) | copy-start | bytes 2359300
  52.8 7.2 %copy-start.10 = (bf16[4,128,128]{2,1,0:T(8,128)(2,1)S(1)}, bf16[4,128,128]{2,1,0:T(8,128)(2,1)}, u32[]{:S(2)}) copy-start(bf16[4,128,128]{2,1,0:T(8,128)(2,1)} %get-tuple-element.13) | copy-start | bytes 393220
  60.0 5.1 %copy-start.9 = (bf16[1,1024,128]{2,1,0:T(8,128)(2,1)}, bf16[1,1024,128]{2,1,0:T(8,128)(2,1)S(1)}, u32[]{:S(2)}) copy-start(bf16[1,1024,128]{2,1,0:T(8,128)(2,1)S(1)} %copy.12) | copy-start | bytes 786436
  65.0 2.3 %copy-start.3 = (bf16[4,128,1024]{1,2,0:T(8,128)(2,1)S(1)}, bf16[4,128,1024]{1,2,0:T(8,128)(2,1)}, u32[]{:S(2)}) copy-start(bf16[4,128,1024]{1,2,0:T(8,128)(2,1)} %copy-done.2) | copy-start | bytes 3145732
  65.0 2.3 %copy-start.8 = (f32[4,128,128]{2,1,0:T(8,128)S(1)}, f32[4,128,128]{2,1,0:T(8,128)}, u32[]{:S(2)}) copy-start(f32[4,128,128]{2,1,0:T(8,128)} %get-tuple-element.12) | copy-start | bytes 786436
  67.3 4.3 %copy-start.5 = (bf16[4,128,1024]{1,2,0:T(8,128)(2,1)S(1)}, bf16[4,128,1024]{1,2,0:T(8,128)(2,1)}, u32[]{:S(2)}) copy-start(bf16[4,128,1024]{1,2,0:T(8,128)(2,1)} %copy-done.4) | copy-start | bytes 3145732
  67.3 4.3 %copy-start.7 = (f32[4,128,128]{2,1,0:T(8,128)S(1)}, f32[4,128,128]{2,1,0:T(8,128)}, u32[]{:S(2)}) copy-start(f32[4,128,128]{2,1,0:T(8,128)} %get-tuple-element.14) | copy-start | bytes 786436
  74.7 116.2 %copy-start.1 = (bf16[512,1024]{1,0:T(8,128)(2,1)S(1)}, bf16[512,1024]{1,0:T(8,128)(2,1)}, u32[]{:S(2)}) copy-start(bf16[512,1024]{1,0:T(8,128)(2,1)} %param.11) | copy-start | bytes 3145732
where the time goes:
time: 221 us
  blocking collectives  133 us (60%)
  matrix products  44 us (20%)
  local copies, waits for them, and re-layouts  14.5 us (7%)
  starting transfers between devices  13.9 us (6%)
  other arithmetic  13.2 us (6%)
    psum x1, blocking collectives, local(): summed = lax.psum(filter_raw, 'seq')  108 us
    psum x1, blocking collectives, local(): energy = lax.psum(jnp.sum(summed * summed), 'tp')  25 us
    dot_general x1, matrix products, local(): jnp.einsum('bgcs,bgis->bgci', grad_lanes, mat_cur, preferred_element_type...  7.43 us
    dot_general x1, matrix products, local(): jnp.dot(merged, diag_table, precision=lax.Precision.HIGHEST, preferred_el...  7.27 us
    dot_general x1, matrix products, local(): jnp.einsum('bgcs,bgis->bgci', grad_after, mat_next, preferred_element_typ...  7.12 us
    ppermute x3, starting transfers between devices, from_behind(): lax.ppermute(value, axis, [(source, source + steps) for source in range(l...  6.22 us
    dot_general x1, matrix products, local(): jnp.einsum('bgcs,bgsi->bgci', prod_lanes, mat_cur, preferred_element_type...  5.9 us
    ppermute x1, starting transfers between devices, with_halo(): lax.ppermute(head, axis, [((i + 1) % count, i) for i in range(ends)])  5.75 us
  transfers between devices with their start and end apart: 5, of which 0 were waited for; matrix products, arithmetic and copies ran while one was open for 20% of the time, Pallas kernels for 0%

commit v1 on v0

v1 whole, which is shorter than its diff:
```python
import functools, math
import jax, jax.numpy as jnp
from jax import lax
from jax.experimental import pallas as pl
from jax.experimental.pallas import tpu as pltpu
from jax.sharding import PartitionSpec as P

BLK = 128
CH = 16
EXTRA = 4
F32, BF16 = jnp.float32, jnp.bfloat16

MESH = pl.DeviceIdType.MESH


def block_docs(ids_ref, blocks):
    first = [ids_ref[BLK * b] for b in range(blocks)]
    last = [ids_ref[BLK * b + BLK - 1] for b in range(blocks)]
    before = [jnp.int32(0)]
    for b in range(blocks):
        before.append(before[-1] + last[b] - first[b])
    return first, last, before


def extra_slot(first, before, blocks, e):
    b_of, doc = jnp.int32(0), first[0] + 1 + e
    for b in range(1, blocks):
        here = before[b] <= e
        b_of = jnp.where(here, b, b_of)
        doc = jnp.where(here, first[b] + 1 + e - before[b], doc)
    return b_of, doc


def main_kernel(blocks, groups,
                ids_ref, q_ref, k_ref, v_ref, c_ref, ph_ref, zh_ref, f_ref, docs_ref, ldocs_ref, rdocs_ref,
                go_ref, gq_ref, gk_ref, gv_ref, part_ref,
                pt, zt, cv, bk, rolled, folded):
    first, last, before = block_docs(ids_ref, blocks)
    total = before[blocks]
    chans = groups * CH
    step = pl.program_id(0)

    def turned(x):
        return x.T

    for b in range(blocks):
        rows = pl.ds(BLK * b, BLK)
        k, v = k_ref[rows, :].astype(F32), v_ref[rows, :].astype(F32)
        pt[b + 1] = turned((k * v).astype(BF16))
        c, q = c_ref[rows, :].astype(F32), q_ref[rows, :].astype(F32)
        zt[b] = turned((c * q).astype(BF16))
    pt[0] = turned(ph_ref[...])
    zt[blocks] = turned(zh_ref[...])

    taps = f_ref[pl.ds(pl.multiple_of(step * groups, groups), groups), :].astype(F32) if f_ref.shape[0] != groups else f_ref[...].astype(F32)
    for s in range(8):
        rolled[pl.ds(s, groups, stride=8), :] = pltpu.roll(taps, s, 1) if s else taps

    row = lax.broadcasted_iota(jnp.int32, (BLK, BLK), 0)
    lane = lax.broadcasted_iota(jnp.int32, (BLK, BLK), 1)
    upper = lane >= row

    def mask_of(docs, doc, on=None):
        m = docs == doc
        if on is not None:
            m = m & on
        return jnp.broadcast_to(m.astype(F32), (CH, BLK)).astype(BF16)

    def one_pass(start, main):
        d = [docs_ref[b:b + 1, :] for b in range(blocks)]
        if main:
            d_prev = [ldocs_ref[...]] + d[:-1]
            d_next = d[1:] + [rdocs_ref[...]]
            m_prev = [mask_of(d_prev[b], first[b]) for b in range(blocks)]
            m_cur = [mask_of(d[b], first[b]) for b in range(blocks)]
            m_last = [mask_of(d[b], last[b]) for b in range(blocks)]
            m_next = [mask_of(d_next[b], last[b]) for b in range(blocks)]
        where_, x_b, y_b, x_m, y_m = [], [], [], [], []
        for e in range(EXTRA):
            b_e, doc_e = extra_slot(first, before, blocks, start + e)
            live = start + e < total
            where_.append(b_e)
            xs = [mask_of(d[b], doc_e, live & (b_e == b)) for b in range(blocks)]
            ys = [mask_of(d[b], doc_e - 1, live & (b_e == b)) for b in range(blocks)]
            x_b.append(xs)
            y_b.append(ys)
            x_m.append(xs[0] + xs[1] + xs[2] + xs[3])
            y_m.append(ys[0] + ys[1] + ys[2] + ys[3])
        nothing = jnp.zeros((CH, BLK), BF16)
        for g in range(groups):
            rows = pl.ds(CH * g, CH)
            base = rolled[pl.ds(8 * g, 8), :]
            ring = jnp.concatenate([pltpu.roll(base, 8 * r, 1) if r else base for r in range(BLK // 8)], axis=0)
            low = jnp.where(upper, ring, 0.0).astype(BF16)
            up = jnp.where(upper, 0.0, ring).astype(BF16)
            p_left, p_here, z_here, z_right, z_pair = [], [], [], [], []
            if main:
                p = [pt[b, rows, :] for b in range(blocks + 1)]
                z = [zt[b, rows, :] for b in range(blocks + 1)]
                for b in range(blocks):
                    p_left.append(p[b] * m_prev[b])
                    p_here.append(p[b + 1] * m_cur[b])
                    z_here.append(z[b] * m_last[b])
                    z_right.append(z[b + 1] * m_next[b])
                    z_pair.append(z[b] * m_cur[b])
            for e in range(EXTRA):
                pe, ze = pt[where_[e] + 1, rows, :], zt[where_[e], rows, :]
                p_left.append(nothing)
                p_here.append(pe * x_m[e])
                z_here.append(ze * y_m[e])
                z_right.append(nothing)
                z_pair.append(ze * x_m[e])
            p_win = jnp.concatenate([jnp.concatenate(p_left, 0), jnp.concatenate(p_here, 0)], 1)
            z_win = jnp.concatenate([jnp.concatenate(z_here, 0), jnp.concatenate(z_right, 0)], 1)
            conv = jnp.dot(p_win, jnp.concatenate([up, low], 0), preferred_element_type=F32).astype(BF16)
            back = lax.dot_general(z_win, jnp.concatenate([low, up], 1), (((1,), (1,)), ((), ())),
                                   preferred_element_type=F32).astype(BF16)
            pair = jnp.dot(jnp.concatenate(z_pair, 0).T, p_win, preferred_element_type=F32)
            off = blocks if main else 0
            for b in range(blocks):
                acc = conv[CH * b:CH * b + CH] * m_cur[b] if main else cv[b, rows, :]
                acb = back[CH * b:CH * b + CH] * m_last[b] if main else bk[b, rows, :]
                for e in range(EXTRA):
                    sl = slice(CH * (off + e), CH * (off + e + 1))
                    acc = acc + conv[sl] * x_b[e][b]
                    acb = acb + back[sl] * y_b[e][b]
                cv[b, rows, :] = acc
                bk[b, rows, :] = acb
            merged = jnp.where(lane <= row, pair[:, BLK:], pair[:, :BLK])
            fold = None if main else folded[pl.ds(8 * g, 8), :]
            for r in range(BLK // 8):
                part = merged[8 * r:8 * r + 8]
                part = pltpu.roll(part, BLK - 8 * r, 1) if r else part
                fold = part if fold is None else fold + part
            folded[pl.ds(8 * g, 8), :] = fold

    one_pass(jnp.int32(0), True)

    def more(p, carry):
        one_pass(p * EXTRA, False)
        return carry

    lax.fori_loop(1, (total + EXTRA - 1) // EXTRA, more, 0)

    raw = folded[pl.ds(0, groups, stride=8), :]
    for i in range(1, 8):
        raw = raw + pltpu.roll(folded[pl.ds(i, groups, stride=8), :], BLK - i, 1)
    flip = (lane == (BLK - row) % BLK).astype(F32)
    raw = jnp.dot(raw, flip, precision=lax.Precision.HIGHEST, preferred_element_type=F32)
    for h in range(groups // 2):
        part_ref[h] = raw[2 * h:2 * h + 2]

    for b in range(blocks):
        rows = pl.ds(BLK * b, BLK)
        conv, back = cv[b].T.astype(F32), bk[b].T.astype(F32)
        go_ref[rows, :] = (q_ref[rows, :].astype(F32) * conv).astype(BF16)
        gq_ref[rows, :] = (c_ref[rows, :].astype(F32) * conv).astype(BF16)
        gk_ref[rows, :] = (v_ref[rows, :].astype(F32) * back).astype(BF16)
        gv_ref[rows, :] = (k_ref[rows, :].astype(F32) * back).astype(BF16)


def main_call(q, k, v, c, ph, zh, filters, ids, docs, ldocs, rdocs, tc=256):
    rows, chans = q.shape
    blocks = rows // BLK
    groups = tc // CH
    tile = pl.BlockSpec((rows, tc), lambda i, ids: (0, i))
    rim = pl.BlockSpec((BLK, tc), lambda i, ids: (0, i))
    whole = lambda a: pl.BlockSpec(a.shape, lambda i, ids: (0,) * a.ndim)
    nat = jax.ShapeDtypeStruct((rows, chans), BF16)
    return pl.pallas_call(
        functools.partial(main_kernel, blocks, groups),
        out_shape=(nat, nat, nat, nat, jax.ShapeDtypeStruct((chans // CH // 2, 2, BLK), F32)),
        grid_spec=pltpu.PrefetchScalarGridSpec(
            num_scalar_prefetch=1,
            grid=(chans // tc,),
            in_specs=[tile] * 4 + [rim] * 2 + [pl.BlockSpec((groups, BLK), lambda i, ids: (i, 0)), whole(docs), whole(ldocs), whole(rdocs)],
            out_specs=[tile] * 4 + [pl.BlockSpec((groups // 2, 2, BLK), lambda i, ids: (i, 0, 0))],
            scratch_shapes=[
                pltpu.VMEM((blocks + 1, tc, BLK), BF16), pltpu.VMEM((blocks + 1, tc, BLK), BF16),
                pltpu.VMEM((blocks, tc, BLK), BF16), pltpu.VMEM((blocks, tc, BLK), BF16),
                pltpu.VMEM((8 * groups, BLK), F32), pltpu.VMEM((8 * groups, BLK), F32),
            ]),
        compiler_params=pltpu.CompilerParams(vmem_limit_bytes=60 * 2**20),
        name="main",
    )(ids, q, k, v, c, ph, zh, filters, docs, ldocs, rdocs)


def halo_kernel(count, q_hbm, k_hbm, v_hbm, c_hbm, docs_ref, ph_ref, zh_ref, ld_ref, rd_ref,
                k_rim, v_rim, q_rim, c_rim, p_out, z_out, ld_in, rd_in, load_sem, send_sem, recv_sem):
    me = lax.axis_index("seq")
    right, left = lax.rem(me + 1, count), lax.rem(me + count - 1, count)
    barrier = pltpu.get_barrier_semaphore()
    for peer in (left, right):
        pl.semaphore_signal(barrier, inc=1, device_id={"seq": peer}, device_id_type=MESH)
    rows = k_hbm.shape[0]
    tail, head = pl.ds(rows - BLK, BLK), pl.ds(0, BLK)
    loads = [pltpu.make_async_copy(src.at[part], dst, load_sem.at[i]) for i, (src, part, dst) in enumerate(
        ((k_hbm, tail, k_rim), (v_hbm, tail, v_rim), (c_hbm, head, c_rim), (q_hbm, head, q_rim)))]
    for load in loads:
        load.start()

    def send(i, src, dst, peer):
        return pltpu.make_async_remote_copy(src_ref=src, dst_ref=dst, send_sem=send_sem.at[i], recv_sem=recv_sem.at[i],
                                            device_id={"seq": peer}, device_id_type=MESH)

    pl.semaphore_wait(barrier, 2)
    blocks = docs_ref.shape[0]
    sends = [send(2, docs_ref.at[pl.ds(blocks - 1, 1)], ld_in, right), send(3, docs_ref.at[pl.ds(0, 1)], rd_in, left)]
    for s in sends:
        s.start()
    loads[0].wait()
    loads[1].wait()
    p_out[...] = (k_rim[...].astype(F32) * v_rim[...].astype(F32)).astype(BF16)
    sends.append(send(0, p_out, ph_ref, right))
    sends[-1].start()
    loads[2].wait()
    loads[3].wait()
    z_out[...] = (c_rim[...].astype(F32) * q_rim[...].astype(F32)).astype(BF16)
    sends.append(send(1, z_out, zh_ref, left))
    sends[-1].start()
    for s in sends:
        s.wait()
    ld_ref[...] = jnp.where(me == 0, -1, ld_in[...])
    rd_ref[...] = jnp.where(me == count - 1, -1, rd_in[...])


def halo_call(count, q, k, v, c, docs):
    chans = q.shape[1]
    rim = pltpu.VMEM((BLK, chans), BF16)
    vm = pl.BlockSpec(memory_space=pltpu.VMEM)
    line = jax.ShapeDtypeStruct((1, BLK), jnp.int32)
    rim_out = jax.ShapeDtypeStruct((BLK, chans), BF16)
    return pl.pallas_call(
        functools.partial(halo_kernel, count),
        out_shape=(rim_out, rim_out, line, line),
        in_specs=[pl.BlockSpec(memory_space=pl.ANY)] * 4 + [vm],
        out_specs=(vm,) * 4,
        scratch_shapes=[rim] * 6 + [pltpu.VMEM((1, BLK), jnp.int32)] * 2
        + [pltpu.SemaphoreType.DMA((4,))] * 3,
        compiler_params=pltpu.CompilerParams(collective_id=0, has_side_effects=True, vmem_limit_bytes=60 * 2**20),
        name="halo",
    )(q, k, v, c, docs)


def sum_kernel(count, wide, bound, part_ref, out_ref, got, own, whole, energy, send_a, recv_a, send_b, recv_b, send_c, recv_c):
    me, tp = lax.axis_index("seq"), lax.axis_index("tp")
    barrier = pltpu.get_barrier_semaphore()

    def seq_peer(d):
        return lax.rem(me + d, count)

    def tp_peer(d):
        return lax.rem(tp + d, wide)

    def each(n, do):
        lax.fori_loop(1, n, lambda d, carry: (do(d), carry)[1], 0)

    each(count, lambda d: pl.semaphore_signal(barrier, inc=1, device_id={"seq": seq_peer(d)}, device_id_type=MESH))
    each(wide, lambda d: pl.semaphore_signal(barrier, inc=1, device_id={"tp": tp_peer(d)}, device_id_type=MESH))
    pl.semaphore_wait(barrier, count + wide - 2)

    def scatter(d):
        return pltpu.make_async_remote_copy(
            src_ref=part_ref.at[seq_peer(d)], dst_ref=got.at[d], send_sem=send_a.at[d], recv_sem=recv_a.at[d],
            device_id={"seq": seq_peer(d)}, device_id_type=MESH)

    def spread(d):
        return pltpu.make_async_remote_copy(
            src_ref=own, dst_ref=whole.at[me], send_sem=send_b.at[d], recv_sem=recv_b.at[d],
            device_id={"seq": seq_peer(d)}, device_id_type=MESH)

    def tell(d):
        return pltpu.make_async_remote_copy(
            src_ref=energy.at[0], dst_ref=energy.at[d], send_sem=send_c.at[d], recv_sem=recv_c.at[d],
            device_id={"tp": tp_peer(d)}, device_id_type=MESH)

    each(count, lambda d: scatter(d).start())
    got[0] = part_ref[me]
    each(count, lambda d: scatter(d).wait_recv())
    mine = jnp.sum(got[...], axis=0)
    own[...] = mine
    each(count, lambda d: spread(d).start())
    whole[me] = mine
    each(count, lambda d: spread(d).wait_recv())
    full = whole[...]
    squares = jnp.sum(full * full, axis=0)
    energy[0] = jnp.sum(squares, axis=0, keepdims=True)
    each(wide, lambda d: tell(d).start())
    each(wide, lambda d: tell(d).wait_recv())
    total = jnp.sum(energy[...])
    norm = jnp.sqrt(jnp.full((1, BLK), total, F32))
    factor = jnp.minimum(1.0, bound / (norm + 1e-06))
    for i in range(count):
        out_ref[2 * i:2 * i + 2, :] = whole[i] * factor
    each(count, lambda d: scatter(d).wait_send())
    each(count, lambda d: spread(d).wait_send())
    each(wide, lambda d: tell(d).wait_send())


def sum_call(count, wide, bound, part):
    vm = pl.BlockSpec(memory_space=pltpu.VMEM)
    n, per, taps = part.shape
    sems = pltpu.SemaphoreType.DMA
    return pl.pallas_call(
        functools.partial(sum_kernel, count, wide, bound),
        out_shape=jax.ShapeDtypeStruct((n * per, taps), F32),
        in_specs=[vm], out_specs=vm,
        scratch_shapes=[pltpu.VMEM((count, per, taps), F32), pltpu.VMEM((per, taps), F32), pltpu.VMEM((count, per, taps), F32),
                        pltpu.VMEM((wide, 1, taps), F32)] + [sems((count,))] * 4 + [sems((wide,))] * 2,
        compiler_params=pltpu.CompilerParams(collective_id=1, has_side_effects=True),
        name="total",
    )(part)


def local(queries, key_inputs, value_inputs, filters, doc_ids, cotangent):
    rows, chans = queries.shape
    groups, taps = filters.shape
    count, wide = lax.axis_size("seq"), lax.axis_size("tp")
    docs = doc_ids.reshape(rows // BLK, BLK)
    ph, zh, ldocs, rdocs = halo_call(count, queries, key_inputs, value_inputs, cotangent, docs)
    *grads, part = main_call(queries, key_inputs, value_inputs, cotangent, ph, zh, filters, doc_ids, docs, ldocs, rdocs)
    bound = 1.5 * math.sqrt(groups * wide * taps * (chans // groups) * rows * count)
    return (*grads, sum_call(count, wide, bound, part))


def solution(mesh):
    cells, bank = P("seq", "tp"), P("tp", None)
    return jax.shard_map(local, mesh=mesh, in_specs=(cells, cells, cells, bank, P("seq"), cells),
                         out_specs=(cells, cells, cells, cells, bank), check_vma=False)
```

time: 221 us -> 52.5 us (0.24)
  the two profiles are of different devices: /device:TPU:128 before, /device:TPU:1 now
where the time goes in v1:
time: 52.5 us; the launch traced here: 52.2 us
  Pallas kernels  50.1 us (95%)
  local copies, waits for them, and re-layouts  1.38 us (3%)
  between operations  0.65 us (1%)
    pallas_call x1, Pallas kernels, sum_call(): pl.pallas_call(functools.partial(sum_kernel, count, wide, bound), out_sha...  28.7 us
    pallas_call x1, Pallas kernels, halo_call(): pl.pallas_call(functools.partial(halo_kernel, count), out_shape=(rim_out,...  11.2 us
    pallas_call x1, Pallas kernels, main_call(): pl.pallas_call(functools.partial(main_kernel, blocks, groups), out_shape=...  10.3 us
    unnamed x1, local copies, waits for them, and re-layouts  1.38 us

profile of v1, /device:TPU:1, one launch (start us, length us, event | category | flops | bytes accessed | tf_op | source)
XLA Modules:
  0.0 52.2 jit_solution(17223915660597428380)
XLA Ops:
  0.6 11.2 %halo.1 = (bf16[128,1024]{1,0:T(8,128)(2,1)}, bf16[128,1024]{1,0:T(8,128)(2,1)}, s32[1,128]{1,0:T(1,128)}, s32[1,128]{1,0:T(1,128)}) custom-call(bf16[512,1024]{1,0:T(8,128)(2,1)} %q_ref.1, bf16[512,1024]{1,0:T(8,128)(2,1)} %k_ref.1, bf16[512,1024]{1,0:T(8,128)(2,1)} %v_ref.1, bf16[512,1024]{1,0:T(8,128)(2,1)} %c_ref.1, s32[4,128]{1,0:T(4,128)} %bitcast.1), custom_call_target="tpu_custom_call" | custom-call | tf_op jit(solution)/shard_map/halo/pallas_call | solution.py:233
  11.8 10.3 %main.1 = (bf16[512,1024]{1,0:T(8,128)(2,1)}, bf16[512,1024]{1,0:T(8,128)(2,1)}, bf16[512,1024]{1,0:T(8,128)(2,1)}, bf16[512,1024]{1,0:T(8,128)(2,1)}, f32[32,2,128]{2,1,0:T(2,128)}) custom-call(s32[512]{0:T(512)} %ids_ref.1, bf16[512,1024]{1,0:T(8,128)(2,1)} %q_ref.1, bf16[512,1024]{1,0:T(8,128)(2,1)} %k_ref.1, bf16[512,1024]{1,0:T(8,128)(2,1)} %v_ref.1, ...), custom_call_target="tpu_custom_call" | custom-call | tf_op jit(solution)/shard_map/main/pallas_call | solution.py:170
  22.1 28.7 %total.1 = f32[64,128]{1,0:T(8,128)} custom-call(f32[32,2,128]{2,1,0:T(2,128)} %get-tuple-element.22.part_ref), custom_call_target="tpu_custom_call" | custom-call | tf_op jit(solution)/shard_map/total/pallas_call | solution.py:304
  50.8 1.4 %copy.12 = f32[64,128]{1,0:T(8,128)} copy(f32[64,128]{1,0:T(8,128)} %total.1) | data formatting | bytes 65536

commit v2 on v1

--- a/solution.py
+++ b/solution.py
@@ -147,8 +147,7 @@
         raw = raw + pltpu.roll(folded[pl.ds(i, groups, stride=8), :], BLK - i, 1)
     flip = (lane == (BLK - row) % BLK).astype(F32)
     raw = jnp.dot(raw, flip, precision=lax.Precision.HIGHEST, preferred_element_type=F32)
-    for h in range(groups // 2):
-        part_ref[h] = raw[2 * h:2 * h + 2]
+    part_ref[...] = raw
 
     for b in range(blocks):
         rows = pl.ds(BLK * b, BLK)
@@ -169,12 +168,12 @@
     nat = jax.ShapeDtypeStruct((rows, chans), BF16)
     return pl.pallas_call(
         functools.partial(main_kernel, blocks, groups),
-        out_shape=(nat, nat, nat, nat, jax.ShapeDtypeStruct((chans // CH // 2, 2, BLK), F32)),
+        out_shape=(nat, nat, nat, nat, jax.ShapeDtypeStruct((chans // CH, BLK), F32)),
         grid_spec=pltpu.PrefetchScalarGridSpec(
             num_scalar_prefetch=1,
             grid=(chans // tc,),
             in_specs=[tile] * 4 + [rim] * 2 + [pl.BlockSpec((groups, BLK), lambda i, ids: (i, 0)), whole(docs), whole(ldocs), whole(rdocs)],
-            out_specs=[tile] * 4 + [pl.BlockSpec((groups // 2, 2, BLK), lambda i, ids: (i, 0, 0))],
+            out_specs=[tile] * 4 + [pl.BlockSpec((groups, BLK), lambda i, ids: (i, 0))],
             scratch_shapes=[
                 pltpu.VMEM((blocks + 1, tc, BLK), BF16), pltpu.VMEM((blocks + 1, tc, BLK), BF16),
                 pltpu.VMEM((blocks, tc, BLK), BF16), pltpu.VMEM((blocks, tc, BLK), BF16),
@@ -242,71 +241,88 @@
     )(q, k, v, c, docs)
 
 
-def sum_kernel(count, wide, bound, part_ref, out_ref, got, own, whole, energy, send_a, recv_a, send_b, recv_b, send_c, recv_c):
+QUAD = 4
+
+
+def remote(src, dst, send_sem, recv_sem, to):
+    return pltpu.make_async_remote_copy(src_ref=src, dst_ref=dst, send_sem=send_sem, recv_sem=recv_sem,
+                                        device_id=to, device_id_type=MESH)
+
+
+def sum_kernel(count, wide, bound, part_ref, out_ref, got, ring, whole, energy,
+               send_a, recv_a, send_b, recv_b, send_c, recv_c, send_d, recv_d):
     me, tp = lax.axis_index("seq"), lax.axis_index("tp")
+    tall = count // QUAD
+    side, up = lax.rem(me, QUAD), me // QUAD
+    slab = part_ref.shape[0] // QUAD
+
+    def near(d):
+        return {"seq": up * QUAD + lax.rem(side + d, QUAD)}
+
+    def far(d):
+        return {"seq": lax.rem(me + QUAD * d, count)}
+
+    def across(d):
+        return {"tp": lax.rem(tp + d, wide)}
+
+    def rows(i):
+        return pl.ds(pl.multiple_of(i * slab, slab), slab)
+
     barrier = pltpu.get_barrier_semaphore()
-
-    def seq_peer(d):
-        return lax.rem(me + d, count)
-
-    def tp_peer(d):
-        return lax.rem(tp + d, wide)
-
-    def each(n, do):
-        lax.fori_loop(1, n, lambda d, carry: (do(d), carry)[1], 0)
-
-    each(count, lambda d: pl.semaphore_signal(barrier, inc=1, device_id={"seq": seq_peer(d)}, device_id_type=MESH))
-    each(wide, lambda d: pl.semaphore_signal(barrier, inc=1, device_id={"tp": tp_peer(d)}, device_id_type=MESH))
-    pl.semaphore_wait(barrier, count + wide - 2)
-
-    def scatter(d):
-        return pltpu.make_async_remote_copy(
-            src_ref=part_ref.at[seq_peer(d)], dst_ref=got.at[d], send_sem=send_a.at[d], recv_sem=recv_a.at[d],
-            device_id={"seq": seq_peer(d)}, device_id_type=MESH)
-
-    def spread(d):
-        return pltpu.make_async_remote_copy(
-            src_ref=own, dst_ref=whole.at[me], send_sem=send_b.at[d], recv_sem=recv_b.at[d],
-            device_id={"seq": seq_peer(d)}, device_id_type=MESH)
-
-    def tell(d):
-        return pltpu.make_async_remote_copy(
-            src_ref=energy.at[0], dst_ref=energy.at[d], send_sem=send_c.at[d], recv_sem=recv_c.at[d],
-            device_id={"tp": tp_peer(d)}, device_id_type=MESH)
-
-    each(count, lambda d: scatter(d).start())
-    got[0] = part_ref[me]
-    each(count, lambda d: scatter(d).wait_recv())
-    mine = jnp.sum(got[...], axis=0)
-    own[...] = mine
-    each(count, lambda d: spread(d).start())
-    whole[me] = mine
-    each(count, lambda d: spread(d).wait_recv())
+    for to, n in ((near, QUAD), (far, tall), (across, wide)):
+        for d in range(1, n):
+            pl.semaphore_signal(barrier, inc=1, device_id=to(d), device_id_type=MESH)
+    pl.semaphore_wait(barrier, QUAD + tall + wide - 3)
+
+    scatter = [remote(part_ref.at[rows(lax.rem(side + d, QUAD))], got.at[d], send_a.at[d], recv_a.at[d], near(d))
+               for d in range(1, QUAD)]
+    climb = [remote(ring.at[up], ring.at[up], send_b.at[d], recv_b.at[d], far(d)) for d in range(1, tall)]
+    spread = [remote(whole.at[rows(side)], whole.at[rows(side)], send_c.at[d], recv_c.at[d], near(d)) for d in range(1, QUAD)]
+    tell = [remote(energy.at[tp], energy.at[tp], send_d.at[d], recv_d.at[d], across(d)) for d in range(1, wide)]
+
+    def start(copies):
+        for copy in copies:
+            copy.start()
+
+    def arrive(copies):
+        for copy in copies:
+            copy.wait_recv()
+
+    start(scatter)
+    mine = part_ref[rows(side), :]
+    arrive(scatter)
+    for d in range(1, QUAD):
+        mine = mine + got[d]
+    ring[up] = mine
+    start(climb)
+    arrive(climb)
+    mine = ring[0]
+    for z in range(1, tall):
+        mine = mine + ring[z]
+    whole[rows(side), :] = mine
+    start(spread)
+    arrive(spread)
     full = whole[...]
-    squares = jnp.sum(full * full, axis=0)
-    energy[0] = jnp.sum(squares, axis=0, keepdims=True)
-    each(wide, lambda d: tell(d).start())
-    each(wide, lambda d: tell(d).wait_recv())
-    total = jnp.sum(energy[...])
-    norm = jnp.sqrt(jnp.full((1, BLK), total, F32))
-    factor = jnp.minimum(1.0, bound / (norm + 1e-06))
-    for i in range(count):
-        out_ref[2 * i:2 * i + 2, :] = whole[i] * factor
-    each(count, lambda d: scatter(d).wait_send())
-    each(count, lambda d: spread(d).wait_send())
-    each(wide, lambda d: tell(d).wait_send())
+    energy[tp] = jnp.sum(full * full, axis=0, keepdims=True)
+    start(tell)
+    arrive(tell)
+    norm = jnp.sqrt(jnp.full((1, BLK), jnp.sum(energy[...]), F32))
+    out_ref[...] = full * jnp.minimum(1.0, bound / (norm + 1e-06))
+    for copy in scatter + climb + spread + tell:
+        copy.wait_send()
 
 
 def sum_call(count, wide, bound, part):
     vm = pl.BlockSpec(memory_space=pltpu.VMEM)
-    n, per, taps = part.shape
-    sems = pltpu.SemaphoreType.DMA
+    slab = (part.shape[0] // QUAD, part.shape[1])
+    tall = count // QUAD
+    sems = [pltpu.SemaphoreType.DMA((n,)) for n in (QUAD, QUAD, tall, tall, QUAD, QUAD, wide, wide)]
     return pl.pallas_call(
         functools.partial(sum_kernel, count, wide, bound),
-        out_shape=jax.ShapeDtypeStruct((n * per, taps), F32),
+        out_shape=jax.ShapeDtypeStruct(part.shape, F32),
         in_specs=[vm], out_specs=vm,
-        scratch_shapes=[pltpu.VMEM((count, per, taps), F32), pltpu.VMEM((per, taps), F32), pltpu.VMEM((count, per, taps), F32),
-                        pltpu.VMEM((wide, 1, taps), F32)] + [sems((count,))] * 4 + [sems((wide,))] * 2,
+        scratch_shapes=[pltpu.VMEM((QUAD, *slab), F32), pltpu.VMEM((tall, *slab), F32), pltpu.VMEM(part.shape, F32),
+                        pltpu.VMEM((wide, 1, part.shape[1]), F32)] + sems,
         compiler_params=pltpu.CompilerParams(collective_id=1, has_side_effects=True),
         name="total",
     )(part)

time: 52.5 us -> 48.9 us (0.931)
  Pallas kernels: 50.1 us -> 46.6 us
    pallas_call x1, Pallas kernels: 28.7 us -> 25.1 us  [sum_call(): pl.pallas_call(functools.partial(sum_kernel, count, wide, bound), out_sha...]
where the time goes in v2:
time: 48.9 us; the launch traced here: 48.6 us
  Pallas kernels  46.6 us (95%)
  local copies, waits for them, and re-layouts  1.38 us (3%)
  between operations  0.65 us (1%)
    pallas_call x1, Pallas kernels, sum_call(): pl.pallas_call(functools.partial(sum_kernel, count, wide, bound), out_sha...  25.1 us
    pallas_call x1, Pallas kernels, halo_call(): pl.pallas_call(functools.partial(halo_kernel, count), out_shape=(rim_out,...  11.2 us
    pallas_call x1, Pallas kernels, main_call(): pl.pallas_call(functools.partial(main_kernel, blocks, groups), out_shape=...  10.3 us
    unnamed x1, local copies, waits for them, and re-layouts  1.38 us

profile of v2, /device:TPU:1, one launch (start us, length us, event | category | flops | bytes accessed | tf_op | source)
XLA Modules:
  0.0 48.6 jit_solution(2537698458570112143)
XLA Ops:
  0.6 11.2 %halo.1 = (bf16[128,1024]{1,0:T(8,128)(2,1)}, bf16[128,1024]{1,0:T(8,128)(2,1)}, s32[1,128]{1,0:T(1,128)}, s32[1,128]{1,0:T(1,128)}) custom-call(bf16[512,1024]{1,0:T(8,128)(2,1)} %q_ref.1, bf16[512,1024]{1,0:T(8,128)(2,1)} %k_ref.1, bf16[512,1024]{1,0:T(8,128)(2,1)} %v_ref.1, bf16[512,1024]{1,0:T(8,128)(2,1)} %c_ref.1, s32[4,128]{1,0:T(4,128)} %bitcast.1), custom_call_target="tpu_custom_call" | custom-call | tf_op jit(solution)/shard_map/halo/pallas_call | solution.py:232
  11.8 10.3 %main.1 = (bf16[512,1024]{1,0:T(8,128)(2,1)}, bf16[512,1024]{1,0:T(8,128)(2,1)}, bf16[512,1024]{1,0:T(8,128)(2,1)}, bf16[512,1024]{1,0:T(8,128)(2,1)}, f32[64,128]{1,0:T(8,128)}) custom-call(s32[512]{0:T(512)} %ids_ref.1, bf16[512,1024]{1,0:T(8,128)(2,1)} %q_ref.1, bf16[512,1024]{1,0:T(8,128)(2,1)} %k_ref.1, bf16[512,1024]{1,0:T(8,128)(2,1)} %v_ref.1, ...), custom_call_target="tpu_custom_call" | custom-call | tf_op jit(solution)/shard_map/main/pallas_call | solution.py:169
  22.1 25.1 %total.1 = f32[64,128]{1,0:T(8,128)} custom-call(f32[64,128]{1,0:T(8,128)} %get-tuple-element.22.part_ref), custom_call_target="tpu_custom_call" | custom-call | tf_op jit(solution)/shard_map/total/pallas_call | solution.py:320
  47.2 1.4 %copy.12 = f32[64,128]{1,0:T(8,128)} copy(f32[64,128]{1,0:T(8,128)} %total.1) | data formatting | bytes 65536

commit v3 on v0

v3 whole, which is shorter than its diff:
```python
import functools, math
import jax, jax.numpy as jnp
from jax import lax
from jax.experimental import pallas as pl
from jax.experimental.pallas import tpu as pltpu
from jax.sharding import PartitionSpec as P

BLK = 128
CH = 16
EXTRA = 4
QUAD = 4
TILE = 256
F32, BF16 = jnp.float32, jnp.bfloat16
MESH = pl.DeviceIdType.MESH


def block_docs(ids_ref, blocks):
    first = [ids_ref[BLK * b] for b in range(blocks)]
    last = [ids_ref[BLK * b + BLK - 1] for b in range(blocks)]
    before = [jnp.int32(0)]
    for b in range(blocks):
        before.append(before[-1] + last[b] - first[b])
    return first, last, before


def extra_slot(first, before, blocks, e):
    b_of, doc = jnp.int32(0), first[0] + 1 + e
    for b in range(1, blocks):
        here = before[b] <= e
        b_of = jnp.where(here, b, b_of)
        doc = jnp.where(here, first[b] + 1 + e - before[b], doc)
    return b_of, doc


def mask_of(docs, doc, on=None):
    m = docs == doc
    if on is not None:
        m = m & on
    return jnp.broadcast_to(m.astype(F32), (CH, BLK)).astype(BF16)


def extra_masks(docs, first, before, blocks, start):
    total = before[blocks]
    out = []
    for e in range(EXTRA):
        b_e, doc_e = extra_slot(first, before, blocks, start + e)
        live = start + e < total
        xs = [mask_of(docs[b], doc_e, live & (b_e == b)) for b in range(blocks)]
        ys = [mask_of(docs[b], doc_e - 1, live & (b_e == b)) for b in range(blocks)]
        out.append((b_e, xs, ys, sum(xs[1:], xs[0]), sum(ys[1:], ys[0])))
    return out


def band_of(base, upper):
    ring = jnp.concatenate([pltpu.roll(base, 8 * r, 1) if r else base for r in range(BLK // 8)], axis=0)
    return jnp.where(upper, ring, 0.0).astype(BF16), jnp.where(upper, 0.0, ring).astype(BF16)


def wide_mul(a, b):
    return (a.astype(F32) * b.astype(F32)).astype(BF16)


def remote(src, dst, send_sem, recv_sem, to):
    return pltpu.make_async_remote_copy(src_ref=src, dst_ref=dst, send_sem=send_sem, recv_sem=recv_sem,
                                        device_id=to, device_id_type=MESH)


def start(copies):
    for copy in copies:
        copy.start()


def arrive(copies):
    for copy in copies:
        copy.wait_recv()


def fused_kernel(count, wide, bound, chans, rows_n,
                 ids_ref, docs_ref, f_ref, q_hbm, k_hbm, v_hbm, c_hbm,
                 go_hbm, gq_hbm, gk_hbm, gv_hbm, sum_ref,
                 q_ref, k_ref, v_ref, c_ref, zn, pt, zt, cv, bk, o_go, o_gq, o_gk, o_gv,
                 p_out, p_in, z_out, z_in, ld_in, rd_in, rolled, folded, same, masks, part, got, ring, whole, energy,
                 rim_sem, load_sem, save_sem, halo_s, halo_r,
                 send_a, recv_a, send_b, recv_b, send_c, recv_c, send_d, recv_d):
    me, tp = lax.axis_index("seq"), lax.axis_index("tp")
    blocks, groups, tiles = rows_n // BLK, chans // CH, chans // TILE
    per = TILE // CH
    tall = count // QUAD
    side, up = lax.rem(me, QUAD), me // QUAD
    slab = groups // QUAD
    right, left = lax.rem(me + 1, count), lax.rem(me + count - 1, count)

    def near(d):
        return {"seq": up * QUAD + lax.rem(side + d, QUAD), "tp": tp}

    def far(d):
        return {"seq": lax.rem(me + QUAD * d, count), "tp": tp}

    def plane(d, e):
        return {"seq": up * QUAD + lax.rem(side + d, QUAD), "tp": lax.rem(tp + e, wide)}

    def slab_rows(i):
        return pl.ds(pl.multiple_of(i * slab, slab), slab)

    tail, head = pl.ds(rows_n - BLK, BLK), pl.ds(0, BLK)
    low_rows, high_rows = pl.ds(0, rows_n - BLK), pl.ds(BLK, rows_n - BLK)
    rims = [pltpu.make_async_copy(src.at[r], dst.at[r], rim_sem.at[i]) for i, (src, dst, r) in enumerate(
        ((k_hbm, k_ref, tail), (v_hbm, v_ref, tail), (c_hbm, c_ref, head), (q_hbm, q_ref, head)))]
    start(rims)
    rest = [pltpu.make_async_copy(src.at[r], dst.at[r], load_sem.at[i]) for i, (src, dst, r) in enumerate(
        ((k_hbm, k_ref, low_rows), (v_hbm, v_ref, low_rows), (c_hbm, c_ref, high_rows), (q_hbm, q_ref, high_rows)))]
    start(rest)

    barrier = pltpu.get_barrier_semaphore()
    others = [plane(d, e) for d in range(QUAD) for e in range(wide) if d or e]
    others += [far(d) for d in range(1, tall)]
    others += [{"seq": left, "tp": tp}, {"seq": right, "tp": tp}]
    for to in others:
        pl.semaphore_signal(barrier, inc=1, device_id=to, device_id_type=MESH)

    halo = [remote(p_out, p_in, halo_s.at[0], halo_r.at[0], {"seq": right, "tp": tp}),
            remote(docs_ref.at[pl.ds(blocks - 1, 1)], ld_in, halo_s.at[1], halo_r.at[1], {"seq": right, "tp": tp}),
            remote(z_out, z_in, halo_s.at[2], halo_r.at[2], {"seq": left, "tp": tp}),
            remote(docs_ref.at[pl.ds(0, 1)], rd_in, halo_s.at[3], halo_r.at[3], {"seq": left, "tp": tp})]
    scatter = [remote(part.at[slab_rows(lax.rem(side + d, QUAD))], got.at[d], send_a.at[d], recv_a.at[d], near(d))
               for d in range(1, QUAD)]
    climb = [remote(ring.at[up], ring.at[up], send_b.at[d], recv_b.at[d], far(d)) for d in range(1, tall)]
    spread = [remote(whole.at[slab_rows(side)], whole.at[slab_rows(side)], send_c.at[d], recv_c.at[d], near(d))
              for d in range(1, QUAD)]
    slot = side * wide + tp
    tell = [remote(energy.at[slot], energy.at[slot], send_d.at[d * wide + e], recv_d.at[d * wide + e], plane(d, e))
            for d in range(QUAD) for e in range(wide) if d or e]

    row = lax.broadcasted_iota(jnp.int32, (BLK, BLK), 0)
    lane = lax.broadcasted_iota(jnp.int32, (BLK, BLK), 1)
    upper = lane >= row
    first, last, before = block_docs(ids_ref, blocks)
    docs = [docs_ref[b:b + 1, :] for b in range(blocks)]
    across = [jnp.broadcast_to(d.astype(F32), (BLK, BLK)) for d in docs]
    down = [a.T for a in across]
    same[0] = jnp.where((lane <= row) & (down[0] == across[0]), 1.0, 0.0)
    for b in range(1, blocks):
        same[b] = jnp.where(down[b] == jnp.where(lane <= row, across[b], across[b - 1]), 1.0, 0.0)
    taps = f_ref[...].astype(F32)
    for s in range(8):
        rolled[pl.ds(s, groups, stride=8), :] = pltpu.roll(taps, s, 1) if s else taps

    for copy in rims:
        copy.wait()
    p_out[...] = wide_mul(k_ref[tail, :], v_ref[tail, :])
    z_out[...] = wide_mul(c_ref[head, :], q_ref[head, :])
    for copy in rest:
        copy.wait()

    def prepare(t, carry):
        cols = pl.ds(pl.multiple_of(t * TILE, TILE), TILE)
        for b in range(blocks):
            r = pl.ds(BLK * b, BLK)
            pt[b + 1, cols, :] = wide_mul(k_ref[r, cols], v_ref[r, cols]).T
            z = wide_mul(c_ref[r, cols], q_ref[r, cols])
            zn[r, cols] = z
            zt[b, cols, :] = z.T
        return carry

    lax.fori_loop(0, tiles, prepare, 0)
    pl.semaphore_wait(barrier, len(others))
    start(halo)

    nothing = jnp.zeros((CH, BLK), BF16)
    octet = BLK // CH

    def fold(acc):
        out = acc[:8]
        for r in range(1, BLK // 8):
            out = out + pltpu.roll(acc[8 * r:8 * r + 8], BLK - 8 * r, 1)
        return out

    def inner_pairs(t, carry):
        cols = pl.ds(pl.multiple_of(t * BLK, BLK), BLK)
        for g in range(octet):
            here = pl.ds(pl.multiple_of(t * BLK + CH * g, CH), CH)
            acc = None
            p = [pt[b, here, :] for b in range(1, blocks + 1)]
            for b in range(blocks):
                pick = jnp.concatenate([p[b - 1], p[b]], 1) if b else p[0]
                zero = jnp.concatenate([nothing, nothing], 1) if b else nothing
                pad = jnp.concatenate([zero] * g + [pick] + [zero] * (octet - 1 - g), 0)
                pair = jnp.dot(zn[pl.ds(BLK * b, BLK), cols], pad, preferred_element_type=F32)
                if b:
                    pair = jnp.where(lane <= row, pair[:, BLK:], pair[:, :BLK])
                pair = pair * same[b]
                acc = pair if acc is None else acc + pair
            folded[pl.ds(pl.multiple_of(t * BLK // 2 + 8 * g, 8), 8), :] = fold(acc)
        return carry

    lax.fori_loop(0, chans // BLK, inner_pairs, 0)

    arrive(halo)
    ldocs = jnp.where(me == 0, -1, ld_in[...])
    rdocs = jnp.where(me == count - 1, -1, rd_in[...])
    same[0] = jnp.where((lane > row) & (down[0] == jnp.broadcast_to(ldocs.astype(F32), (BLK, BLK))), 1.0, 0.0)

    def rim_pairs(t, carry):
        cols = pl.ds(pl.multiple_of(t * BLK, BLK), BLK)
        turned = p_in[:, cols].T
        pt[0, cols, :] = turned
        zt[blocks, cols, :] = z_in[:, cols].T
        for g in range(0, octet, 2):
            a, b = turned[CH * g:CH * g + CH], turned[CH * g + CH:CH * g + 2 * CH]
            zero = jnp.concatenate([nothing, nothing], 1)
            pad = jnp.concatenate([zero] * g + [jnp.concatenate([a, nothing], 1), jnp.concatenate([nothing, b], 1)]
                                  + [zero] * (octet - 2 - g), 0)
            pair = jnp.dot(zn[pl.ds(0, BLK), cols], pad, preferred_element_type=F32)
            for i in range(2):
                at = pl.ds(pl.multiple_of(t * BLK // 2 + 8 * (g + i), 8), 8)
                folded[at, :] = folded[at, :] + fold(pair[:, BLK * i:BLK * i + BLK] * same[0])
        return carry

    lax.fori_loop(0, chans // BLK, rim_pairs, 0)
    raw = folded[pl.ds(0, groups, stride=8), :]
    for i in range(1, 8):
        raw = raw + pltpu.roll(folded[pl.ds(i, groups, stride=8), :], BLK - i, 1)
    part[...] = raw
    start(scatter)

    d_prev, d_next = [ldocs] + docs[:-1], docs[1:] + [rdocs]
    m_prev = [mask_of(d_prev[b], first[b]) for b in range(blocks)]
    m_cur = [mask_of(docs[b], first[b]) for b in range(blocks)]
    m_last = [mask_of(docs[b], last[b]) for b in range(blocks)]
    m_next = [mask_of(d_next[b], last[b]) for b in range(blocks)]
    extras = extra_masks(docs, first, before, blocks, 0)
    flat = m_prev + m_cur + m_last + m_next
    for _, xs, ys, x, y in extras:
        flat += xs + ys + [x, y]
    for i, m in enumerate(flat):
        masks[i] = m

    def gates(t):
        def load(i):
            return masks[i]
        m_prev, m_cur, m_last, m_next = [[load(k * blocks + b) for b in range(blocks)] for k in range(4)]
        base_i, size = 4 * blocks, 2 * blocks + 2
        cols = pl.ds(t * TILE, TILE) if isinstance(t, int) else pl.ds(pl.multiple_of(t * TILE, TILE), TILE)
        for g in range(per):
            here = pl.ds(t * TILE + CH * g, CH) if isinstance(t, int) else pl.ds(pl.multiple_of(t * TILE + CH * g, CH), CH)
            at8 = pl.ds(t * (TILE // 2) + 8 * g, 8) if isinstance(t, int) else pl.ds(pl.multiple_of(t * (TILE // 2) + 8 * g, 8), 8)
            local = pl.ds(CH * g, CH)
            low, high = band_of(rolled[at8, :], upper)
            p = [pt[b, here, :] for b in range(blocks + 1)]
            z = [zt[b, here, :] for b in range(blocks + 1)]
            p_left = [p[b] * m_prev[b] for b in range(blocks)]
            p_here = [p[b + 1] * m_cur[b] for b in range(blocks)]
            z_here = [z[b] * m_last[b] for b in range(blocks)]
            z_right = [z[b + 1] * m_next[b] for b in range(blocks)]
            for e in range(EXTRA):
                b_e = extras[e][0]
                p_left.append(nothing)
                p_here.append(pt[b_e + 1, here, :] * load(base_i + e * size + 2 * blocks))
                z_here.append(zt[b_e, here, :] * load(base_i + e * size + 2 * blocks + 1))
                z_right.append(nothing)
            p_win = jnp.concatenate([jnp.concatenate(p_left, 0), jnp.concatenate(p_here, 0)], 1)
            z_win = jnp.concatenate([jnp.concatenate(z_here, 0), jnp.concatenate(z_right, 0)], 1)
            conv = jnp.dot(p_win, jnp.concatenate([high, low], 0), preferred_element_type=F32).astype(BF16)
            back = lax.dot_general(z_win, jnp.concatenate([low, high], 1), (((1,), (1,)), ((), ())),
                                   preferred_element_type=F32).astype(BF16)
            for b in range(blocks):
                acc = conv[CH * b:CH * b + CH] * m_cur[b]
                acb = back[CH * b:CH * b + CH] * m_last[b]
                for e in range(EXTRA):
                    sl = slice(CH * (blocks + e), CH * (blocks + e + 1))
                    acc = acc + conv[sl] * load(base_i + e * size + b)
                    acb = acb + back[sl] * load(base_i + e * size + blocks + b)
                cv[b, local, :] = acc
                bk[b, local, :] = acb
        for b in range(blocks):
            r = pl.ds(BLK * b, BLK)
            conv, back = cv[b].T.astype(F32), bk[b].T.astype(F32)
            o_go[r, cols] = (q_ref[r, cols].astype(F32) * conv).astype(BF16)
            o_gq[r, cols] = (c_ref[r, cols].astype(F32) * conv).astype(BF16)
            o_gk[r, cols] = (v_ref[r, cols].astype(F32) * back).astype(BF16)
            o_gv[r, cols] = (k_ref[r, cols].astype(F32) * back).astype(BF16)

    def saves(t):
        cols = pl.ds(t * TILE, TILE)
        return [pltpu.make_async_copy(src.at[:, cols], dst.at[:, cols], save_sem.at[t, i]) for i, (src, dst) in enumerate(
            ((o_go, go_hbm), (o_gq, gq_hbm), (o_gk, gk_hbm), (o_gv, gv_hbm)))]

    cut = tiles // 2

    def run(a, b):
        lax.fori_loop(a, b, lambda t, carry: (gates(t), carry)[1], 0)
        for t in range(a, b):
            start(saves(t))

    run(0, cut)
    arrive(scatter)
    mine = part[slab_rows(side), :]
    for d in range(1, QUAD):
        mine = mine + got[d]
    ring[up] = mine
    start(climb)
    run(cut, tiles)
    arrive(climb)
    mine = ring[0]
    for z in range(1, tall):
        mine = mine + ring[z]
    whole[slab_rows(side), :] = mine
    energy[slot] = jnp.sum(mine * mine, axis=0, keepdims=True)
    start(tell)
    start(spread)
    for t in range(tiles):
        for copy in saves(t):
            copy.wait()
    for copy in halo + scatter + climb:
        copy.wait_send()
    arrive(tell)
    arrive(spread)
    norm = jnp.sqrt(jnp.full((1, BLK), jnp.sum(energy[...]), F32))
    sum_ref[...] = whole[...] * jnp.minimum(1.0, bound / (norm + 1e-06))
    for copy in tell + spread:
        copy.wait_send()


def fused_call(count, wide, bound, q, k, v, c, filters, ids, docs):
    rows, chans = q.shape
    blocks, groups, tiles = rows // BLK, chans // CH, chans // TILE
    tall = count // QUAD
    vm, hbm = pl.BlockSpec(memory_space=pltpu.VMEM), pl.BlockSpec(memory_space=pl.ANY)
    nat = jax.ShapeDtypeStruct((rows, chans), BF16)
    dma = lambda *n: pltpu.SemaphoreType.DMA(n)
    big = pltpu.VMEM((rows, chans), BF16)
    rim = pltpu.VMEM((BLK, chans), BF16)
    line = pltpu.VMEM((1, BLK), jnp.int32)
    n_masks = 4 * blocks + EXTRA * (2 * blocks + 2)
    slab = groups // QUAD
    return pl.pallas_call(
        functools.partial(fused_kernel, count, wide, bound, chans, rows),
        out_shape=(nat, nat, nat, nat, jax.ShapeDtypeStruct((groups, BLK), F32)),
        in_specs=[pl.BlockSpec(memory_space=pltpu.SMEM), vm, vm] + [hbm] * 4,
        out_specs=(hbm,) * 4 + (vm,),
        scratch_shapes=[big] * 5 + [pltpu.VMEM((blocks + 1, chans, BLK), BF16)] * 2 + [pltpu.VMEM((blocks, TILE, BLK), BF16)] * 2
        + [big] * 4 + [rim] * 4 + [line] * 2
        + [pltpu.VMEM((8 * groups, BLK), F32)] * 2 + [pltpu.VMEM((blocks, BLK, BLK), F32), pltpu.VMEM((n_masks, CH, BLK), BF16),
           pltpu.VMEM((groups, BLK), F32), pltpu.VMEM((QUAD, slab, BLK), F32), pltpu.VMEM((tall, slab, BLK), F32),
           pltpu.VMEM((groups, BLK), F32), pltpu.VMEM((QUAD * wide, 1, BLK), F32)]
        + [dma(4), dma(4), dma(tiles, 4), dma(4), dma(4),
           dma(QUAD), dma(QUAD), dma(tall), dma(tall), dma(QUAD), dma(QUAD), dma(QUAD * wide), dma(QUAD * wide)],
        compiler_params=pltpu.CompilerParams(collective_id=0, has_side_effects=True, vmem_limit_bytes=60 * 2**20),
        cost_estimate=pl.CostEstimate(flops=2 * 10**9, bytes_accessed=8 * 2**20, transcendentals=0),
        name="fused",
    )(ids, docs, filters, q, k, v, c)


def finish_kernel(blocks, ids_ref, docs_ref, f_ref, total_ref, a_go, a_gq, a_gk, a_gv, q_hbm, k_hbm, v_hbm, c_hbm,
                  go_ref, gq_ref, gk_ref, gv_ref, sum_ref,
                  q_ref, k_ref, v_ref, c_ref, pt, zt, cv, bk, rolled, load_sem):
    step = pl.program_id(0)
    per = TILE // CH
    first, last, before = block_docs(ids_ref, blocks)
    total = before[blocks]
    row = lax.broadcasted_iota(jnp.int32, (BLK, BLK), 0)
    lane = lax.broadcasted_iota(jnp.int32, (BLK, BLK), 1)
    go_ref[...], gq_ref[...], gk_ref[...], gv_ref[...] = a_go[...], a_gq[...], a_gk[...], a_gv[...]

    @pl.when(step == 0)
    def _():
        flip = (lane == (BLK - row) % BLK).astype(F32)
        sum_ref[...] = jnp.dot(total_ref[...], flip, precision=lax.Precision.HIGHEST, preferred_element_type=F32)

    @pl.when(total > EXTRA)
    def _():
        cols = pl.ds(pl.multiple_of(step * TILE, TILE), TILE)
        loads = [pltpu.make_async_copy(src.at[:, cols], dst, load_sem.at[i]) for i, (src, dst) in enumerate(
            ((q_hbm, q_ref), (k_hbm, k_ref), (v_hbm, v_ref), (c_hbm, c_ref)))]
        for copy in loads:
            copy.start()
        for copy in loads:
            copy.wait()
        for b in range(blocks):
            r = pl.ds(BLK * b, BLK)
            pt[b] = wide_mul(k_ref[r, :], v_ref[r, :]).T
            zt[b] = wide_mul(c_ref[r, :], q_ref[r, :]).T
        cv[...] = jnp.zeros(cv.shape, BF16)
        bk[...] = jnp.zeros(bk.shape, BF16)
        taps = f_ref[...].astype(F32)
        for s in range(8):
            rolled[pl.ds(s, per, stride=8), :] = pltpu.roll(taps, s, 1) if s else taps
        docs = [docs_ref[b:b + 1, :] for b in range(blocks)]
        upper = lane >= row

        def more(p, carry):
            extras = extra_masks(docs, first, before, blocks, p * EXTRA)
            for g in range(per):
                here = pl.ds(CH * g, CH)
                low, _ = band_of(rolled[pl.ds(8 * g, 8), :], upper)
                p_here = jnp.concatenate([pt[x[0], here, :] * x[3] for x in extras], 0)
                z_here = jnp.concatenate([zt[x[0], here, :] * x[4] for x in extras], 0)
                conv = jnp.dot(p_here, low, preferred_element_type=F32).astype(BF16)
                back = lax.dot_general(z_here, low, (((1,), (1,)), ((), ())), preferred_element_type=F32).astype(BF16)
                for b in range(blocks):
                    acc, acb = cv[b, here, :], bk[b, here, :]
                    for e, x in enumerate(extras):
                        sl = slice(CH * e, CH * (e + 1))
                        acc = acc + conv[sl] * x[1][b]
                        acb = acb + back[sl] * x[2][b]
                    cv[b, here, :] = acc
                    bk[b, here, :] = acb
            return carry

        lax.fori_loop(1, (total + EXTRA - 1) // EXTRA, more, 0)
        for b in range(blocks):
            r = pl.ds(BLK * b, BLK)
            conv, back = cv[b].T.astype(F32), bk[b].T.astype(F32)
            go_ref[r, :] += (q_ref[r, :].astype(F32) * conv).astype(BF16)
            gq_ref[r, :] += (c_ref[r, :].astype(F32) * conv).astype(BF16)
            gk_ref[r, :] += (v_ref[r, :].astype(F32) * back).astype(BF16)
            gv_ref[r, :] += (k_ref[r, :].astype(F32) * back).astype(BF16)


def finish_call(grads, total, q, k, v, c, filters, ids, docs):
    rows, chans = q.shape
    blocks, per = rows // BLK, TILE // CH
    tile = pl.BlockSpec((rows, TILE), lambda i, ids: (0, i))
    whole = lambda a: pl.BlockSpec(a.shape, lambda i, ids: (0,) * a.ndim)
    hbm = pl.BlockSpec(memory_space=pl.ANY)
    nat = jax.ShapeDtypeStruct((rows, chans), BF16)
    cell = pltpu.VMEM((rows, TILE), BF16)
    turned = pltpu.VMEM((blocks, TILE, BLK), BF16)
    return pl.pallas_call(
        functools.partial(finish_kernel, blocks),
        out_shape=(nat, nat, nat, nat, jax.ShapeDtypeStruct(total.shape, F32)),
        grid_spec=pltpu.PrefetchScalarGridSpec(
            num_scalar_prefetch=1, grid=(chans // TILE,),
            in_specs=[whole(docs), pl.BlockSpec((per, BLK), lambda i, ids: (i, 0)), whole(total)] + [tile] * 4 + [hbm] * 4,
            out_specs=[tile] * 4 + [whole(total)],
            scratch_shapes=[cell] * 4 + [turned] * 4 + [pltpu.VMEM((8 * per, BLK), F32), pltpu.SemaphoreType.DMA((4,))]),
        compiler_params=pltpu.CompilerParams(vmem_limit_bytes=60 * 2**20),
        name="finish",
    )(ids, docs, filters, total, *grads, q, k, v, c)


def local(queries, key_inputs, value_inputs, filters, doc_ids, cotangent):
    rows, chans = queries.shape
    groups, taps = filters.shape
    count, wide = lax.axis_size("seq"), lax.axis_size("tp")
    docs = doc_ids.reshape(rows // BLK, BLK)
    bound = 1.5 * math.sqrt(groups * wide * taps * (chans // groups) * rows * count)
    *grads, total = fused_call(count, wide, bound, queries, key_inputs, value_inputs, cotangent, filters, doc_ids, docs)
    return finish_call(grads, total, queries, key_inputs, value_inputs, cotangent, filters, doc_ids, docs)


def solution(mesh):
    cells, bank = P("seq", "tp"), P("tp", None)
    return jax.shard_map(local, mesh=mesh, in_specs=(cells, cells, cells, bank, P("seq"), cells),
                         out_specs=(cells, cells, cells, cells, bank), check_vma=False)
```

time: 221 us -> 43.4 us (0.20)
  the two profiles are of different devices: /device:TPU:128 before, /device:TPU:1 now
where the time goes in v3:
time: 43.4 us; the launch traced here: 43.2 us
  Pallas kernels  42.5 us (98%)
  between operations  0.64 us (1%)
    pallas_call x1, Pallas kernels, fused_call(): pl.pallas_call(functools.partial(fused_kernel, count, wide, bound, chans,...  36.7 us
    pallas_call x1, Pallas kernels, finish_call(): pl.pallas_call(functools.partial(finish_kernel, blocks), out_shape=(nat,...  5.81 us

profile of v3, /device:TPU:1, one launch (start us, length us, event | category | flops | bytes accessed | tf_op | source)
XLA Modules:
  0.0 43.2 jit_solution(10805907452411604961)
XLA Ops:
  0.6 36.7 %fused.1 = (bf16[512,1024]{1,0:T(8,128)(2,1)}, bf16[512,1024]{1,0:T(8,128)(2,1)}, bf16[512,1024]{1,0:T(8,128)(2,1)}, bf16[512,1024]{1,0:T(8,128)(2,1)}, f32[64,128]{1,0:T(8,128)}) custom-call(s32[512]{0:T(512)} %ids_ref.3, s32[4,128]{1,0:T(4,128)} %bitcast.1, bf16[64,128]{1,0:T(8,128)(2,1)} %f_ref.3, bf16[512,1024]{1,0:T(8,128)(2,1)} %q_hbm.3, ...), custom_call_target="tpu_custom_call" | custom-call | flops 2000000000 | bytes 8388608 | tf_op jit(solution)/shard_map/fused/pallas_call | solution.py:336
  37.4 5.8 %finish.1 = (bf16[512,1024]{1,0:T(8,128)(2,1)}, bf16[512,1024]{1,0:T(8,128)(2,1)}, bf16[512,1024]{1,0:T(8,128)(2,1)}, bf16[512,1024]{1,0:T(8,128)(2,1)}, f32[64,128]{1,0:T(8,128)}) custom-call(s32[512]{0:T(512)} %ids_ref.3, s32[4,128]{1,0:T(4,128)} %bitcast.2, bf16[64,128]{1,0:T(8,128)(2,1)} %f_ref.3, f32[64,128]{1,0:T(8,128)} %get-tuple-element.10.total_ref, ...), custom_call_target="tpu_custom_call" | custom-call | tf_op jit(solution)/shard_map/finish/pallas_call | solution.py:429

commit v4 on v3

--- a/solution.py
+++ b/solution.py
@@ -10,13 +10,15 @@
 EXTRA = 4
 QUAD = 4
 TILE = 256
+FUSED_VMEM = 49 * 2**20
+FINISH_VMEM = 49 * 2**20
 F32, BF16 = jnp.float32, jnp.bfloat16
 MESH = pl.DeviceIdType.MESH
 
 
 def block_docs(ids_ref, blocks):
-    first = [ids_ref[BLK * b] for b in range(blocks)]
-    last = [ids_ref[BLK * b + BLK - 1] for b in range(blocks)]
+    first = [ids_ref[b, 0] for b in range(blocks)]
+    last = [ids_ref[b, BLK - 1] for b in range(blocks)]
     before = [jnp.int32(0)]
     for b in range(blocks):
         before.append(before[-1] + last[b] - first[b])
@@ -102,26 +104,30 @@
     def slab_rows(i):
         return pl.ds(pl.multiple_of(i * slab, slab), slab)
 
+    barrier = pltpu.get_barrier_semaphore()
+    others = [far(d) for d in range(1, tall)]
+    others += [plane(d, e) for d in range(QUAD) for e in range(wide) if d or e]
+    others += [{"seq": left, "tp": tp}, {"seq": right, "tp": tp}]
+    for to in others:
+        pl.semaphore_signal(barrier, inc=1, device_id=to, device_id_type=MESH)
+
     tail, head = pl.ds(rows_n - BLK, BLK), pl.ds(0, BLK)
     low_rows, high_rows = pl.ds(0, rows_n - BLK), pl.ds(BLK, rows_n - BLK)
     rims = [pltpu.make_async_copy(src.at[r], dst.at[r], rim_sem.at[i]) for i, (src, dst, r) in enumerate(
-        ((k_hbm, k_ref, tail), (v_hbm, v_ref, tail), (c_hbm, c_ref, head), (q_hbm, q_ref, head)))]
+        ((c_hbm, c_ref, head), (q_hbm, q_ref, head), (k_hbm, k_ref, tail), (v_hbm, v_ref, tail)))]
     start(rims)
     rest = [pltpu.make_async_copy(src.at[r], dst.at[r], load_sem.at[i]) for i, (src, dst, r) in enumerate(
         ((k_hbm, k_ref, low_rows), (v_hbm, v_ref, low_rows), (c_hbm, c_ref, high_rows), (q_hbm, q_ref, high_rows)))]
     start(rest)
 
-    barrier = pltpu.get_barrier_semaphore()
-    others = [plane(d, e) for d in range(QUAD) for e in range(wide) if d or e]
-    others += [far(d) for d in range(1, tall)]
-    others += [{"seq": left, "tp": tp}, {"seq": right, "tp": tp}]
-    for to in others:
-        pl.semaphore_signal(barrier, inc=1, device_id=to, device_id_type=MESH)
-
-    halo = [remote(p_out, p_in, halo_s.at[0], halo_r.at[0], {"seq": right, "tp": tp}),
-            remote(docs_ref.at[pl.ds(blocks - 1, 1)], ld_in, halo_s.at[1], halo_r.at[1], {"seq": right, "tp": tp}),
-            remote(z_out, z_in, halo_s.at[2], halo_r.at[2], {"seq": left, "tp": tp}),
-            remote(docs_ref.at[pl.ds(0, 1)], rd_in, halo_s.at[3], halo_r.at[3], {"seq": left, "tp": tp})]
+    def tile_cols(t):
+        return pl.ds(t * TILE, TILE)
+
+    to_left, to_right = {"seq": left, "tp": tp}, {"seq": right, "tp": tp}
+    halo_z = [remote(z_out.at[:, tile_cols(t)], z_in.at[:, tile_cols(t)], halo_s.at[t], halo_r.at[t], to_left) for t in range(tiles)]
+    halo_d = remote(docs_ref.at[pl.ds(0, 1)], rd_in, halo_s.at[tiles], halo_r.at[tiles], to_left)
+    halo_p = [remote(p_out, p_in, halo_s.at[tiles + 1], halo_r.at[tiles + 1], to_right),
+              remote(docs_ref.at[pl.ds(blocks - 1, 1)], ld_in, halo_s.at[tiles + 2], halo_r.at[tiles + 2], to_right)]
     scatter = [remote(part.at[slab_rows(lax.rem(side + d, QUAD))], got.at[d], send_a.at[d], recv_a.at[d], near(d))
                for d in range(1, QUAD)]
     climb = [remote(ring.at[up], ring.at[up], send_b.at[d], recv_b.at[d], far(d)) for d in range(1, tall)]
@@ -137,18 +143,23 @@
     first, last, before = block_docs(ids_ref, blocks)
     docs = [docs_ref[b:b + 1, :] for b in range(blocks)]
     across = [jnp.broadcast_to(d.astype(F32), (BLK, BLK)) for d in docs]
-    down = [a.T for a in across]
-    same[0] = jnp.where((lane <= row) & (down[0] == across[0]), 1.0, 0.0)
-    for b in range(1, blocks):
-        same[b] = jnp.where(down[b] == jnp.where(lane <= row, across[b], across[b - 1]), 1.0, 0.0)
-    taps = f_ref[...].astype(F32)
+    for b in range(blocks):
+        same[b] = jnp.where((lane <= row) & (across[b].T == across[b]), 1.0, 0.0)
+    taps = f_ref[0].astype(F32)
     for s in range(8):
         rolled[pl.ds(s, groups, stride=8), :] = pltpu.roll(taps, s, 1) if s else taps
-
-    for copy in rims:
+    m_cur = [mask_of(docs[b], first[b]) for b in range(blocks)]
+    for b in range(blocks):
+        masks[blocks + b] = m_cur[b]
+    for b in range(1, blocks):
+        masks[b] = mask_of(docs[b - 1], first[b])
+
+    for copy in rims[:2]:
+        copy.wait()
+    z_out[...] = wide_mul(c_ref[head, :], q_ref[head, :])
+    for copy in rims[2:]:
         copy.wait()
     p_out[...] = wide_mul(k_ref[tail, :], v_ref[tail, :])
-    z_out[...] = wide_mul(c_ref[head, :], q_ref[head, :])
     for copy in rest:
         copy.wait()
 
@@ -164,10 +175,16 @@
 
     lax.fori_loop(0, tiles, prepare, 0)
     pl.semaphore_wait(barrier, len(others))
-    start(halo)
+    halo_d.start()
+    start(halo_z)
+    start(halo_p)
 
     nothing = jnp.zeros((CH, BLK), BF16)
+    zero = jnp.concatenate([nothing, nothing], 1)
     octet = BLK // CH
+
+    def beside(a, b):
+        return [jnp.concatenate([a, nothing], 1), jnp.concatenate([nothing, b], 1)]
 
     def fold(acc):
         out = acc[:8]
@@ -175,71 +192,79 @@
             out = out + pltpu.roll(acc[8 * r:8 * r + 8], BLK - 8 * r, 1)
         return out
 
+    def spot(t, g):
+        return pl.multiple_of(t * TILE + CH * g, CH), pl.multiple_of(t * (TILE // 2) + 8 * g, 8)
+
     def inner_pairs(t, carry):
-        cols = pl.ds(pl.multiple_of(t * BLK, BLK), BLK)
-        for g in range(octet):
-            here = pl.ds(pl.multiple_of(t * BLK + CH * g, CH), CH)
-            acc = None
-            p = [pt[b, here, :] for b in range(1, blocks + 1)]
+        for g in range(0, per, 2):
+            h, k = g // octet, g % octet
+            cols = pl.ds(pl.multiple_of(t * TILE + BLK * h, BLK), BLK)
+            here = [pl.ds(spot(t, g + i)[0], CH) for i in range(2)]
+            left_z, left_p = [], []
+            for i in range(2):
+                for b in range(1, blocks):
+                    left_z.append(zt[b, here[i], :] * masks[blocks + b])
+                    p = pt[b, here[i], :] * masks[b]
+                    left_p.append(jnp.concatenate([nothing, p] if i else [p, nothing], 1))
+                left_z.append(nothing)
+                left_p.append(zero)
+            prev = jnp.dot(jnp.concatenate(left_z, 0).T, jnp.concatenate(left_p, 0), preferred_element_type=F32)
+            acc = [jnp.where(lane > row, prev[:, BLK * i:BLK * i + BLK], 0.0) for i in range(2)]
             for b in range(blocks):
-                pick = jnp.concatenate([p[b - 1], p[b]], 1) if b else p[0]
-                zero = jnp.concatenate([nothing, nothing], 1) if b else nothing
-                pad = jnp.concatenate([zero] * g + [pick] + [zero] * (octet - 1 - g), 0)
+                pad = jnp.concatenate([zero] * k + beside(pt[b + 1, here[0], :], pt[b + 1, here[1], :])
+                                      + [zero] * (octet - 2 - k), 0)
                 pair = jnp.dot(zn[pl.ds(BLK * b, BLK), cols], pad, preferred_element_type=F32)
-                if b:
-                    pair = jnp.where(lane <= row, pair[:, BLK:], pair[:, :BLK])
-                pair = pair * same[b]
-                acc = pair if acc is None else acc + pair
-            folded[pl.ds(pl.multiple_of(t * BLK // 2 + 8 * g, 8), 8), :] = fold(acc)
+                acc = [acc[i] + pair[:, BLK * i:BLK * i + BLK] * same[b] for i in range(2)]
+            for i in range(2):
+                folded[pl.ds(spot(t, g + i)[1], 8), :] = fold(acc[i])
         return carry
 
-    lax.fori_loop(0, chans // BLK, inner_pairs, 0)
-
-    arrive(halo)
-    ldocs = jnp.where(me == 0, -1, ld_in[...])
+    lax.fori_loop(0, tiles, inner_pairs, 0)
+
+    halo_d.wait_recv()
     rdocs = jnp.where(me == count - 1, -1, rd_in[...])
-    same[0] = jnp.where((lane > row) & (down[0] == jnp.broadcast_to(ldocs.astype(F32), (BLK, BLK))), 1.0, 0.0)
-
-    def rim_pairs(t, carry):
-        cols = pl.ds(pl.multiple_of(t * BLK, BLK), BLK)
-        turned = p_in[:, cols].T
-        pt[0, cols, :] = turned
-        zt[blocks, cols, :] = z_in[:, cols].T
-        for g in range(0, octet, 2):
-            a, b = turned[CH * g:CH * g + CH], turned[CH * g + CH:CH * g + 2 * CH]
-            zero = jnp.concatenate([nothing, nothing], 1)
-            pad = jnp.concatenate([zero] * g + [jnp.concatenate([a, nothing], 1), jnp.concatenate([nothing, b], 1)]
-                                  + [zero] * (octet - 2 - g), 0)
-            pair = jnp.dot(zn[pl.ds(0, BLK), cols], pad, preferred_element_type=F32)
+    beyond = jnp.broadcast_to(rdocs.astype(F32), (BLK, BLK)).T
+    same[0] = jnp.where((lane > row) & (beyond == across[blocks - 1]), 1.0, 0.0)
+    for t in range(tiles):
+        halo_z[t].wait_recv()
+        for g in range(0, per, 2):
+            h, k = g // octet, g % octet
+            cols = pl.ds(t * TILE + BLK * h, BLK)
+            here = [pl.ds(t * TILE + CH * (g + i), CH) for i in range(2)]
+            pad = jnp.concatenate([zero] * k + beside(pt[blocks, here[0], :], pt[blocks, here[1], :])
+                                  + [zero] * (octet - 2 - k), 0)
+            pair = jnp.dot(z_in[:, cols], pad, preferred_element_type=F32)
             for i in range(2):
-                at = pl.ds(pl.multiple_of(t * BLK // 2 + 8 * (g + i), 8), 8)
+                at = pl.ds(t * (TILE // 2) + 8 * (g + i), 8)
                 folded[at, :] = folded[at, :] + fold(pair[:, BLK * i:BLK * i + BLK] * same[0])
-        return carry
-
-    lax.fori_loop(0, chans // BLK, rim_pairs, 0)
     raw = folded[pl.ds(0, groups, stride=8), :]
     for i in range(1, 8):
         raw = raw + pltpu.roll(folded[pl.ds(i, groups, stride=8), :], BLK - i, 1)
     part[...] = raw
     start(scatter)
+    arrive(halo_p)
+    ldocs = jnp.where(me == 0, -1, ld_in[...])
 
     d_prev, d_next = [ldocs] + docs[:-1], docs[1:] + [rdocs]
-    m_prev = [mask_of(d_prev[b], first[b]) for b in range(blocks)]
-    m_cur = [mask_of(docs[b], first[b]) for b in range(blocks)]
+    m_prev = [mask_of(d_prev[0], first[0])]
     m_last = [mask_of(docs[b], last[b]) for b in range(blocks)]
     m_next = [mask_of(d_next[b], last[b]) for b in range(blocks)]
     extras = extra_masks(docs, first, before, blocks, 0)
-    flat = m_prev + m_cur + m_last + m_next
+    masks[0] = m_prev[0]
+    flat = m_last + m_next
     for _, xs, ys, x, y in extras:
         flat += xs + ys + [x, y]
     for i, m in enumerate(flat):
-        masks[i] = m
+        masks[2 * blocks + i] = m
 
     def gates(t):
         def load(i):
             return masks[i]
         m_prev, m_cur, m_last, m_next = [[load(k * blocks + b) for b in range(blocks)] for k in range(4)]
         base_i, size = 4 * blocks, 2 * blocks + 2
+        c2 = pl.ds(pl.multiple_of(t * TILE, TILE), TILE)
+        pt[0, c2, :] = p_in[:, c2].T
+        zt[blocks, c2, :] = z_in[:, c2].T
         cols = pl.ds(t * TILE, TILE) if isinstance(t, int) else pl.ds(pl.multiple_of(t * TILE, TILE), TILE)
         for g in range(per):
             here = pl.ds(t * TILE + CH * g, CH) if isinstance(t, int) else pl.ds(pl.multiple_of(t * TILE + CH * g, CH), CH)
@@ -306,12 +331,12 @@
         mine = mine + ring[z]
     whole[slab_rows(side), :] = mine
     energy[slot] = jnp.sum(mine * mine, axis=0, keepdims=True)
+    start(spread)
     start(tell)
-    start(spread)
     for t in range(tiles):
         for copy in saves(t):
             copy.wait()
-    for copy in halo + scatter + climb:
+    for copy in halo_z + [halo_d] + halo_p + scatter + climb:
         copy.wait_send()
     arrive(tell)
     arrive(spread)
@@ -321,11 +346,12 @@
         copy.wait_send()
 
 
-def fused_call(count, wide, bound, q, k, v, c, filters, ids, docs):
+def fused_call(count, wide, bound, q, k, v, c, filters, docs):
     rows, chans = q.shape
     blocks, groups, tiles = rows // BLK, chans // CH, chans // TILE
     tall = count // QUAD
-    vm, hbm = pl.BlockSpec(memory_space=pltpu.VMEM), pl.BlockSpec(memory_space=pl.ANY)
+    vm, anywhere = pl.BlockSpec(memory_space=pltpu.VMEM), pl.BlockSpec(memory_space=pl.ANY)
+    hbm = pl.BlockSpec(memory_space=pltpu.HBM)
     nat = jax.ShapeDtypeStruct((rows, chans), BF16)
     dma = lambda *n: pltpu.SemaphoreType.DMA(n)
     big = pltpu.VMEM((rows, chans), BF16)
@@ -337,41 +363,45 @@
         functools.partial(fused_kernel, count, wide, bound, chans, rows),
         out_shape=(nat, nat, nat, nat, jax.ShapeDtypeStruct((groups, BLK), F32)),
         in_specs=[pl.BlockSpec(memory_space=pltpu.SMEM), vm, vm] + [hbm] * 4,
-        out_specs=(hbm,) * 4 + (vm,),
+        out_specs=(anywhere,) * 4 + (vm,),
         scratch_shapes=[big] * 5 + [pltpu.VMEM((blocks + 1, chans, BLK), BF16)] * 2 + [pltpu.VMEM((blocks, TILE, BLK), BF16)] * 2
         + [big] * 4 + [rim] * 4 + [line] * 2
         + [pltpu.VMEM((8 * groups, BLK), F32)] * 2 + [pltpu.VMEM((blocks, BLK, BLK), F32), pltpu.VMEM((n_masks, CH, BLK), BF16),
            pltpu.VMEM((groups, BLK), F32), pltpu.VMEM((QUAD, slab, BLK), F32), pltpu.VMEM((tall, slab, BLK), F32),
            pltpu.VMEM((groups, BLK), F32), pltpu.VMEM((QUAD * wide, 1, BLK), F32)]
-        + [dma(4), dma(4), dma(tiles, 4), dma(4), dma(4),
+        + [dma(4), dma(4), dma(tiles, 4), dma(tiles + 3), dma(tiles + 3),
            dma(QUAD), dma(QUAD), dma(tall), dma(tall), dma(QUAD), dma(QUAD), dma(QUAD * wide), dma(QUAD * wide)],
-        compiler_params=pltpu.CompilerParams(collective_id=0, has_side_effects=True, vmem_limit_bytes=60 * 2**20),
+        compiler_params=pltpu.CompilerParams(collective_id=0, has_side_effects=True, vmem_limit_bytes=FUSED_VMEM),
         cost_estimate=pl.CostEstimate(flops=2 * 10**9, bytes_accessed=8 * 2**20, transcendentals=0),
         name="fused",
-    )(ids, docs, filters, q, k, v, c)
-
-
-def finish_kernel(blocks, ids_ref, docs_ref, f_ref, total_ref, a_go, a_gq, a_gk, a_gv, q_hbm, k_hbm, v_hbm, c_hbm,
-                  go_ref, gq_ref, gk_ref, gv_ref, sum_ref,
-                  q_ref, k_ref, v_ref, c_ref, pt, zt, cv, bk, rolled, load_sem):
-    step = pl.program_id(0)
+    )(docs, docs, filters, q, k, v, c)
+
+
+def finish_kernel(blocks, tiles, ids_ref, docs_ref, f_ref, total_ref, a_go, a_gq, a_gk, a_gv, q_hbm, k_hbm, v_hbm, c_hbm,
+                  go_hbm, gq_hbm, gk_hbm, gv_hbm, sum_ref,
+                  q_ref, k_ref, v_ref, c_ref, go_ref, gq_ref, gk_ref, gv_ref, pt, zt, cv, bk, rolled, copy_sem, load_sem):
     per = TILE // CH
+    rows = a_go.shape[0]
+    half = rows // 2
+    results = ((a_go, go_hbm), (a_gq, gq_hbm), (a_gk, gk_hbm), (a_gv, gv_hbm))
+    copies = [pltpu.make_async_copy(src.at[pl.ds(h * half, half)], dst.at[pl.ds(h * half, half)], copy_sem.at[i, h])
+              for i, (src, dst) in enumerate(results) for h in range(2)]
+    for copy in copies:
+        copy.start()
     first, last, before = block_docs(ids_ref, blocks)
     total = before[blocks]
     row = lax.broadcasted_iota(jnp.int32, (BLK, BLK), 0)
     lane = lax.broadcasted_iota(jnp.int32, (BLK, BLK), 1)
-    go_ref[...], gq_ref[...], gk_ref[...], gv_ref[...] = a_go[...], a_gq[...], a_gk[...], a_gv[...]
-
-    @pl.when(step == 0)
-    def _():
-        flip = (lane == (BLK - row) % BLK).astype(F32)
-        sum_ref[...] = jnp.dot(total_ref[...], flip, precision=lax.Precision.HIGHEST, preferred_element_type=F32)
-
-    @pl.when(total > EXTRA)
-    def _():
+    flip = (lane == (BLK - row) % BLK).astype(F32)
+    sum_ref[...] = jnp.dot(total_ref[...], flip, precision=lax.Precision.HIGHEST, preferred_element_type=F32)
+    for copy in copies:
+        copy.wait()
+
+    def add_extras(step, carry):
         cols = pl.ds(pl.multiple_of(step * TILE, TILE), TILE)
         loads = [pltpu.make_async_copy(src.at[:, cols], dst, load_sem.at[i]) for i, (src, dst) in enumerate(
-            ((q_hbm, q_ref), (k_hbm, k_ref), (v_hbm, v_ref), (c_hbm, c_ref)))]
+            ((q_hbm, q_ref), (k_hbm, k_ref), (v_hbm, v_ref), (c_hbm, c_ref),
+             (a_go, go_ref), (a_gq, gq_ref), (a_gk, gk_ref), (a_gv, gv_ref)))]
         for copy in loads:
             copy.start()
         for copy in loads:
@@ -382,7 +412,7 @@
             zt[b] = wide_mul(c_ref[r, :], q_ref[r, :]).T
         cv[...] = jnp.zeros(cv.shape, BF16)
         bk[...] = jnp.zeros(bk.shape, BF16)
-        taps = f_ref[...].astype(F32)
+        taps = f_ref[0, pl.ds(pl.multiple_of(step * per, per), per), :].astype(F32)
         for s in range(8):
             rolled[pl.ds(s, per, stride=8), :] = pltpu.roll(taps, s, 1) if s else taps
         docs = [docs_ref[b:b + 1, :] for b in range(blocks)]
@@ -415,28 +445,35 @@
             gq_ref[r, :] += (c_ref[r, :].astype(F32) * conv).astype(BF16)
             gk_ref[r, :] += (v_ref[r, :].astype(F32) * back).astype(BF16)
             gv_ref[r, :] += (k_ref[r, :].astype(F32) * back).astype(BF16)
-
-
-def finish_call(grads, total, q, k, v, c, filters, ids, docs):
+        stores = [pltpu.make_async_copy(src, dst.at[:, cols], load_sem.at[i]) for i, (src, dst) in enumerate(
+            ((go_ref, go_hbm), (gq_ref, gq_hbm), (gk_ref, gk_hbm), (gv_ref, gv_hbm)))]
+        for copy in stores:
+            copy.start()
+        for copy in stores:
+            copy.wait()
+        return carry
+
+    lax.fori_loop(0, jnp.where(total > EXTRA, tiles, 0), add_extras, 0)
+
+
+def finish_call(grads, total, q, k, v, c, filters, docs):
     rows, chans = q.shape
     blocks, per = rows // BLK, TILE // CH
-    tile = pl.BlockSpec((rows, TILE), lambda i, ids: (0, i))
-    whole = lambda a: pl.BlockSpec(a.shape, lambda i, ids: (0,) * a.ndim)
-    hbm = pl.BlockSpec(memory_space=pl.ANY)
+    vm, anywhere = pl.BlockSpec(memory_space=pltpu.VMEM), pl.BlockSpec(memory_space=pl.ANY)
+    hbm = pl.BlockSpec(memory_space=pltpu.HBM)
     nat = jax.ShapeDtypeStruct((rows, chans), BF16)
     cell = pltpu.VMEM((rows, TILE), BF16)
     turned = pltpu.VMEM((blocks, TILE, BLK), BF16)
     return pl.pallas_call(
-        functools.partial(finish_kernel, blocks),
+        functools.partial(finish_kernel, blocks, chans // TILE),
         out_shape=(nat, nat, nat, nat, jax.ShapeDtypeStruct(total.shape, F32)),
-        grid_spec=pltpu.PrefetchScalarGridSpec(
-            num_scalar_prefetch=1, grid=(chans // TILE,),
-            in_specs=[whole(docs), pl.BlockSpec((per, BLK), lambda i, ids: (i, 0)), whole(total)] + [tile] * 4 + [hbm] * 4,
-            out_specs=[tile] * 4 + [whole(total)],
-            scratch_shapes=[cell] * 4 + [turned] * 4 + [pltpu.VMEM((8 * per, BLK), F32), pltpu.SemaphoreType.DMA((4,))]),
-        compiler_params=pltpu.CompilerParams(vmem_limit_bytes=60 * 2**20),
+        in_specs=[pl.BlockSpec(memory_space=pltpu.SMEM), vm, vm, vm] + [anywhere] * 4 + [hbm] * 4,
+        out_specs=(hbm,) * 4 + (vm,),
+        scratch_shapes=[cell] * 8 + [turned] * 4 + [pltpu.VMEM((8 * per, BLK), F32),
+                                                    pltpu.SemaphoreType.DMA((4, 2)), pltpu.SemaphoreType.DMA((8,))],
+        compiler_params=pltpu.CompilerParams(vmem_limit_bytes=FINISH_VMEM),
         name="finish",
-    )(ids, docs, filters, total, *grads, q, k, v, c)
+    )(docs, docs, filters, total, *grads, q, k, v, c)
 
 
 def local(queries, key_inputs, value_inputs, filters, doc_ids, cotangent):
@@ -444,9 +481,10 @@
     groups, taps = filters.shape
     count, wide = lax.axis_size("seq"), lax.axis_size("tp")
     docs = doc_ids.reshape(rows // BLK, BLK)
+    bank = filters.reshape(1, groups, taps)
     bound = 1.5 * math.sqrt(groups * wide * taps * (chans // groups) * rows * count)
-    *grads, total = fused_call(count, wide, bound, queries, key_inputs, value_inputs, cotangent, filters, doc_ids, docs)
-    return finish_call(grads, total, queries, key_inputs, value_inputs, cotangent, filters, doc_ids, docs)
+    *grads, total = fused_call(count, wide, bound, queries, key_inputs, value_inputs, cotangent, bank, docs)
+    return finish_call(grads, total, queries, key_inputs, value_inputs, cotangent, bank, docs)
 
 
 def solution(mesh):

time: 43.4 us -> 38.3 us (0.88)
  Pallas kernels: 42.5 us -> 36.1 us
  local copies, waits for them, and re-layouts: 0 us -> 1.39 us
    pallas_call x1, Pallas kernels: 36.7 us -> 32.7 us  [fused_call(): pl.pallas_call(functools.partial(fused_kernel, count, wide, bound, chans,...]
    pallas_call x1, Pallas kernels: 5.81 us -> 3.34 us  [finish_call(): pl.pallas_call(functools.partial(finish_kernel, blocks, chans // TILE), o...]
    unnamed x0 -> x4, local copies, waits for them, and re-layouts: none -> 1.39 us
where the time goes in v4:
time: 38.3 us; the launch traced here: 38.1 us
  Pallas kernels  36.1 us (94%)
  local copies, waits for them, and re-layouts  1.39 us (4%)
  between operations  0.65 us (2%)
    pallas_call x1, Pallas kernels, fused_call(): pl.pallas_call(functools.partial(fused_kernel, count, wide, bound, chans,...  32.7 us
    pallas_call x1, Pallas kernels, finish_call(): pl.pallas_call(functools.partial(finish_kernel, blocks, chans // TILE), o...  3.34 us
    unnamed x4, local copies, waits for them, and re-layouts  1.39 us

profile of v4, /device:TPU:1, one launch (start us, length us, event | category | flops | bytes accessed | tf_op | source)
XLA Modules:
  0.0 38.1 jit_solution(16170402425475436188)
XLA Ops:
  0.6 0.0 copy-start.1
  0.6 0.7 %copy-done.1 = s32[512]{0:T(512)S(1)} copy-done((s32[512]{0:T(512)S(1)}, s32[512]{0:T(512)}, u32[]{:S(2)}) %copy-start.1) | copy-done | bytes 2072
  1.3 0.0 copy-start
  1.3 0.7 %copy-done = bf16[64,128]{1,0:T(8,128)(2,1)S(1)} copy-done((bf16[64,128]{1,0:T(8,128)(2,1)S(1)}, bf16[64,128]{1,0:T(8,128)(2,1)}, u32[]{:S(2)}) %copy-start) | copy-done | bytes 16408
  2.0 32.7 %fused.1 = (bf16[512,1024]{1,0:T(8,128)(2,1)S(1)}, bf16[512,1024]{1,0:T(8,128)(2,1)S(1)}, bf16[512,1024]{1,0:T(8,128)(2,1)S(1)}, bf16[512,1024]{1,0:T(8,128)(2,1)S(1)}, f32[64,128]{1,0:T(8,128)S(1)}) custom-call(s32[4,128]{1,0:T(4,128)S(1)} %bitcast.4, s32[4,128]{1,0:T(4,128)S(1)} %bitcast.5, bf16[1,64,128]{2,1,0:T(8,128)(2,1)S(1)} %bitcast.2, ...), custom_call_target="tpu_custom_call" | custom-call | flops 2000000000 | bytes 8388608 | tf_op jit(solution)/shard_map/fused/pallas_call | solution.py:362
  34.7 3.3 %finish.1 = (bf16[512,1024]{1,0:T(8,128)(2,1)}, bf16[512,1024]{1,0:T(8,128)(2,1)}, bf16[512,1024]{1,0:T(8,128)(2,1)}, bf16[512,1024]{1,0:T(8,128)(2,1)}, f32[64,128]{1,0:T(8,128)}) custom-call(s32[4,128]{1,0:T(4,128)S(1)} %bitcast.6, s32[4,128]{1,0:T(4,128)S(1)} %bitcast.7, bf16[1,64,128]{2,1,0:T(8,128)(2,1)S(1)} %bitcast.3, ...), custom_call_target="tpu_custom_call" | custom-call | tf_op jit(solution)/shard_map/finish/pallas_call | solution.py:467
Async XLA Ops:
  0.6 0.7 %copy-start.1 = (s32[512]{0:T(512)S(1)}, s32[512]{0:T(512)}, u32[]{:S(2)}) copy-start(s32[512]{0:T(512)} %param.10) | copy-start | bytes 6148
  1.3 0.7 %copy-start = (bf16[64,128]{1,0:T(8,128)(2,1)S(1)}, bf16[64,128]{1,0:T(8,128)(2,1)}, u32[]{:S(2)}) copy-start(bf16[64,128]{1,0:T(8,128)(2,1)} %param.9) | copy-start | bytes 49156

commit v5 on v4

--- a/solution.py
+++ b/solution.py
@@ -78,11 +78,11 @@
 
 
 def fused_kernel(count, wide, bound, chans, rows_n,
-                 ids_ref, docs_ref, f_ref, q_hbm, k_hbm, v_hbm, c_hbm,
+                 docs_hbm, f_hbm, q_hbm, k_hbm, v_hbm, c_hbm,
                  go_hbm, gq_hbm, gk_hbm, gv_hbm, sum_ref,
-                 q_ref, k_ref, v_ref, c_ref, zn, pt, zt, cv, bk, o_go, o_gq, o_gk, o_gv,
+                 ids_ref, docs_ref, f_ref, q_ref, k_ref, v_ref, c_ref, zn, pt, zt, cv, bk, o_go, o_gq, o_gk, o_gv,
                  p_out, p_in, z_out, z_in, ld_in, rd_in, rolled, folded, same, masks, part, got, ring, whole, energy,
-                 rim_sem, load_sem, save_sem, halo_s, halo_r,
+                 small_sem, rim_sem, load_sem, save_sem, halo_s, halo_r,
                  send_a, recv_a, send_b, recv_b, send_c, recv_c, send_d, recv_d):
     me, tp = lax.axis_index("seq"), lax.axis_index("tp")
     blocks, groups, tiles = rows_n // BLK, chans // CH, chans // TILE
@@ -111,11 +111,15 @@
     for to in others:
         pl.semaphore_signal(barrier, inc=1, device_id=to, device_id_type=MESH)
 
+    small = [pltpu.make_async_copy(src, dst, small_sem.at[i]) for i, (src, dst) in enumerate(
+        ((docs_hbm, ids_ref), (docs_hbm, docs_ref), (f_hbm, f_ref)))]
     tail, head = pl.ds(rows_n - BLK, BLK), pl.ds(0, BLK)
     low_rows, high_rows = pl.ds(0, rows_n - BLK), pl.ds(BLK, rows_n - BLK)
     rims = [pltpu.make_async_copy(src.at[r], dst.at[r], rim_sem.at[i]) for i, (src, dst, r) in enumerate(
         ((c_hbm, c_ref, head), (q_hbm, q_ref, head), (k_hbm, k_ref, tail), (v_hbm, v_ref, tail)))]
-    start(rims)
+    start(rims[:2])
+    start(small)
+    start(rims[2:])
     rest = [pltpu.make_async_copy(src.at[r], dst.at[r], load_sem.at[i]) for i, (src, dst, r) in enumerate(
         ((k_hbm, k_ref, low_rows), (v_hbm, v_ref, low_rows), (c_hbm, c_ref, high_rows), (q_hbm, q_ref, high_rows)))]
     start(rest)
@@ -140,6 +144,8 @@
     row = lax.broadcasted_iota(jnp.int32, (BLK, BLK), 0)
     lane = lax.broadcasted_iota(jnp.int32, (BLK, BLK), 1)
     upper = lane >= row
+    for copy in small:
+        copy.wait()
     first, last, before = block_docs(ids_ref, blocks)
     docs = [docs_ref[b:b + 1, :] for b in range(blocks)]
     across = [jnp.broadcast_to(d.astype(F32), (BLK, BLK)) for d in docs]
@@ -177,7 +183,6 @@
     pl.semaphore_wait(barrier, len(others))
     halo_d.start()
     start(halo_z)
-    start(halo_p)
 
     nothing = jnp.zeros((CH, BLK), BF16)
     zero = jnp.concatenate([nothing, nothing], 1)
@@ -220,6 +225,7 @@
         return carry
 
     lax.fori_loop(0, tiles, inner_pairs, 0)
+    start(halo_p)
 
     halo_d.wait_recv()
     rdocs = jnp.where(me == count - 1, -1, rd_in[...])
@@ -242,15 +248,11 @@
         raw = raw + pltpu.roll(folded[pl.ds(i, groups, stride=8), :], BLK - i, 1)
     part[...] = raw
     start(scatter)
-    arrive(halo_p)
-    ldocs = jnp.where(me == 0, -1, ld_in[...])
-
-    d_prev, d_next = [ldocs] + docs[:-1], docs[1:] + [rdocs]
-    m_prev = [mask_of(d_prev[0], first[0])]
+
+    d_next = docs[1:] + [rdocs]
     m_last = [mask_of(docs[b], last[b]) for b in range(blocks)]
     m_next = [mask_of(d_next[b], last[b]) for b in range(blocks)]
     extras = extra_masks(docs, first, before, blocks, 0)
-    masks[0] = m_prev[0]
     flat = m_last + m_next
     for _, xs, ys, x, y in extras:
         flat += xs + ys + [x, y]
@@ -317,14 +319,15 @@
         for t in range(a, b):
             start(saves(t))
 
-    run(0, cut)
     arrive(scatter)
     mine = part[slab_rows(side), :]
     for d in range(1, QUAD):
         mine = mine + got[d]
     ring[up] = mine
     start(climb)
-    run(cut, tiles)
+    arrive(halo_p)
+    masks[0] = mask_of(jnp.where(me == 0, -1, ld_in[...]), first[0])
+    run(0, cut)
     arrive(climb)
     mine = ring[0]
     for z in range(1, tall):
@@ -333,6 +336,7 @@
     energy[slot] = jnp.sum(mine * mine, axis=0, keepdims=True)
     start(spread)
     start(tell)
+    run(cut, tiles)
     for t in range(tiles):
         for copy in saves(t):
             copy.wait()
@@ -362,24 +366,25 @@
     return pl.pallas_call(
         functools.partial(fused_kernel, count, wide, bound, chans, rows),
         out_shape=(nat, nat, nat, nat, jax.ShapeDtypeStruct((groups, BLK), F32)),
-        in_specs=[pl.BlockSpec(memory_space=pltpu.SMEM), vm, vm] + [hbm] * 4,
+        in_specs=[anywhere] * 2 + [hbm] * 4,
         out_specs=(anywhere,) * 4 + (vm,),
-        scratch_shapes=[big] * 5 + [pltpu.VMEM((blocks + 1, chans, BLK), BF16)] * 2 + [pltpu.VMEM((blocks, TILE, BLK), BF16)] * 2
+        scratch_shapes=[pltpu.SMEM(docs.shape, jnp.int32), pltpu.VMEM(docs.shape, jnp.int32), pltpu.VMEM(filters.shape, BF16)]
+        + [big] * 5 + [pltpu.VMEM((blocks + 1, chans, BLK), BF16)] * 2 + [pltpu.VMEM((blocks, TILE, BLK), BF16)] * 2
         + [big] * 4 + [rim] * 4 + [line] * 2
         + [pltpu.VMEM((8 * groups, BLK), F32)] * 2 + [pltpu.VMEM((blocks, BLK, BLK), F32), pltpu.VMEM((n_masks, CH, BLK), BF16),
            pltpu.VMEM((groups, BLK), F32), pltpu.VMEM((QUAD, slab, BLK), F32), pltpu.VMEM((tall, slab, BLK), F32),
            pltpu.VMEM((groups, BLK), F32), pltpu.VMEM((QUAD * wide, 1, BLK), F32)]
-        + [dma(4), dma(4), dma(tiles, 4), dma(tiles + 3), dma(tiles + 3),
+        + [dma(3), dma(4), dma(4), dma(tiles, 4), dma(tiles + 3), dma(tiles + 3),
            dma(QUAD), dma(QUAD), dma(tall), dma(tall), dma(QUAD), dma(QUAD), dma(QUAD * wide), dma(QUAD * wide)],
         compiler_params=pltpu.CompilerParams(collective_id=0, has_side_effects=True, vmem_limit_bytes=FUSED_VMEM),
         cost_estimate=pl.CostEstimate(flops=2 * 10**9, bytes_accessed=8 * 2**20, transcendentals=0),
         name="fused",
-    )(docs, docs, filters, q, k, v, c)
-
-
-def finish_kernel(blocks, tiles, ids_ref, docs_ref, f_ref, total_ref, a_go, a_gq, a_gk, a_gv, q_hbm, k_hbm, v_hbm, c_hbm,
-                  go_hbm, gq_hbm, gk_hbm, gv_hbm, sum_ref,
-                  q_ref, k_ref, v_ref, c_ref, go_ref, gq_ref, gk_ref, gv_ref, pt, zt, cv, bk, rolled, copy_sem, load_sem):
+    )(docs, filters, q, k, v, c)
+
+
+def finish_kernel(blocks, tiles, docs_hbm, f_hbm, total_hbm, a_go, a_gq, a_gk, a_gv, q_hbm, k_hbm, v_hbm, c_hbm,
+                  go_hbm, gq_hbm, gk_hbm, gv_hbm, sum_hbm,
+                  ids_ref, docs_ref, f_ref, total_ref, sum_ref, small_sem, q_ref, k_ref, v_ref, c_ref, go_ref, gq_ref, gk_ref, gv_ref, pt, zt, cv, bk, rolled, copy_sem, load_sem):
     per = TILE // CH
     rows = a_go.shape[0]
     half = rows // 2
@@ -388,12 +393,21 @@
               for i, (src, dst) in enumerate(results) for h in range(2)]
     for copy in copies:
         copy.start()
-    first, last, before = block_docs(ids_ref, blocks)
-    total = before[blocks]
+    small = [pltpu.make_async_copy(src, dst, small_sem.at[i]) for i, (src, dst) in enumerate(
+        ((total_hbm, total_ref), (docs_hbm, ids_ref), (docs_hbm, docs_ref), (f_hbm, f_ref)))]
+    start(small)
     row = lax.broadcasted_iota(jnp.int32, (BLK, BLK), 0)
     lane = lax.broadcasted_iota(jnp.int32, (BLK, BLK), 1)
     flip = (lane == (BLK - row) % BLK).astype(F32)
+    small[0].wait()
     sum_ref[...] = jnp.dot(total_ref[...], flip, precision=lax.Precision.HIGHEST, preferred_element_type=F32)
+    save = pltpu.make_async_copy(sum_ref, sum_hbm, small_sem.at[4])
+    save.start()
+    for copy in small[1:]:
+        copy.wait()
+    first, last, before = block_docs(ids_ref, blocks)
+    total = before[blocks]
+    save.wait()
     for copy in copies:
         copy.wait()
 
@@ -459,21 +473,21 @@
 def finish_call(grads, total, q, k, v, c, filters, docs):
     rows, chans = q.shape
     blocks, per = rows // BLK, TILE // CH
-    vm, anywhere = pl.BlockSpec(memory_space=pltpu.VMEM), pl.BlockSpec(memory_space=pl.ANY)
-    hbm = pl.BlockSpec(memory_space=pltpu.HBM)
+    anywhere, hbm = pl.BlockSpec(memory_space=pl.ANY), pl.BlockSpec(memory_space=pltpu.HBM)
     nat = jax.ShapeDtypeStruct((rows, chans), BF16)
     cell = pltpu.VMEM((rows, TILE), BF16)
     turned = pltpu.VMEM((blocks, TILE, BLK), BF16)
     return pl.pallas_call(
         functools.partial(finish_kernel, blocks, chans // TILE),
         out_shape=(nat, nat, nat, nat, jax.ShapeDtypeStruct(total.shape, F32)),
-        in_specs=[pl.BlockSpec(memory_space=pltpu.SMEM), vm, vm, vm] + [anywhere] * 4 + [hbm] * 4,
-        out_specs=(hbm,) * 4 + (vm,),
-        scratch_shapes=[cell] * 8 + [turned] * 4 + [pltpu.VMEM((8 * per, BLK), F32),
+        in_specs=[anywhere] * 7 + [hbm] * 4,
+        out_specs=(hbm,) * 5,
+        scratch_shapes=[pltpu.SMEM(docs.shape, jnp.int32), pltpu.VMEM(docs.shape, jnp.int32), pltpu.VMEM(filters.shape, BF16),
+                        pltpu.VMEM(total.shape, F32), pltpu.VMEM(total.shape, F32), pltpu.SemaphoreType.DMA((5,))] + [cell] * 8 + [turned] * 4 + [pltpu.VMEM((8 * per, BLK), F32),
                                                     pltpu.SemaphoreType.DMA((4, 2)), pltpu.SemaphoreType.DMA((8,))],
         compiler_params=pltpu.CompilerParams(vmem_limit_bytes=FINISH_VMEM),
         name="finish",
-    )(docs, docs, filters, total, *grads, q, k, v, c)
+    )(docs, filters, total, *grads, q, k, v, c)
 
 
 def local(queries, key_inputs, value_inputs, filters, doc_ids, cotangent):

time: 38.3 us -> 36 us (0.940)
  Pallas kernels: 36.1 us -> 33.8 us
    pallas_call x1, Pallas kernels: 3.34 us -> 2.2 us  [finish_call(): pl.pallas_call(functools.partial(finish_kernel, blocks, chans // TILE), o...]
    pallas_call x1, Pallas kernels: 32.7 us -> 31.6 us  [fused_call(): pl.pallas_call(functools.partial(fused_kernel, count, wide, bound, chans,...]
where the time goes in v5:
time: 36 us; the launch traced here: 35.9 us
  Pallas kernels  33.8 us (94%)
  local copies, waits for them, and re-layouts  1.39 us (4%)
  between operations  0.65 us (2%)
    pallas_call x1, Pallas kernels, fused_call(): pl.pallas_call(functools.partial(fused_kernel, count, wide, bound, chans,...  31.6 us
    pallas_call x1, Pallas kernels, finish_call(): pl.pallas_call(functools.partial(finish_kernel, blocks, chans // TILE), o...  2.2 us
    unnamed x4, local copies, waits for them, and re-layouts  1.39 us

profile of v5, /device:TPU:1, one launch (start us, length us, event | category | flops | bytes accessed | tf_op | source)
XLA Modules:
  0.0 35.9 jit_solution(17462436184317903401)
XLA Ops:
  0.6 0.0 copy-start.1
  0.6 0.7 %copy-done.1 = s32[512]{0:T(512)S(1)} copy-done((s32[512]{0:T(512)S(1)}, s32[512]{0:T(512)}, u32[]{:S(2)}) %copy-start.1) | copy-done | bytes 2072
  1.3 0.0 copy-start
  1.3 0.7 %copy-done = bf16[64,128]{1,0:T(8,128)(2,1)S(1)} copy-done((bf16[64,128]{1,0:T(8,128)(2,1)S(1)}, bf16[64,128]{1,0:T(8,128)(2,1)}, u32[]{:S(2)}) %copy-start) | copy-done | bytes 16408
  2.0 31.6 %fused.1 = (bf16[512,1024]{1,0:T(8,128)(2,1)S(1)}, bf16[512,1024]{1,0:T(8,128)(2,1)S(1)}, bf16[512,1024]{1,0:T(8,128)(2,1)S(1)}, bf16[512,1024]{1,0:T(8,128)(2,1)S(1)}, f32[64,128]{1,0:T(8,128)S(1)}) custom-call(s32[4,128]{1,0:T(4,128)S(1)} %bitcast.4, bf16[1,64,128]{2,1,0:T(8,128)(2,1)S(1)} %bitcast.2, bf16[512,1024]{1,0:T(8,128)(2,1)} %q_hbm.3, ...), custom_call_target="tpu_custom_call" | custom-call | flops 2000000000 | bytes 8388608 | tf_op jit(solution)/shard_map/fused/pallas_call | solution.py:366
  33.7 2.2 %finish.1 = (bf16[512,1024]{1,0:T(8,128)(2,1)}, bf16[512,1024]{1,0:T(8,128)(2,1)}, bf16[512,1024]{1,0:T(8,128)(2,1)}, bf16[512,1024]{1,0:T(8,128)(2,1)}, f32[64,128]{1,0:T(8,128)}) custom-call(s32[4,128]{1,0:T(4,128)S(1)} %bitcast.5, bf16[1,64,128]{2,1,0:T(8,128)(2,1)S(1)} %bitcast.3, f32[64,128]{1,0:T(8,128)S(1)} %get-tuple-element.10.total_hbm, ...), custom_call_target="tpu_custom_call" | custom-call | tf_op jit(solution)/shard_map/finish/pallas_call | solution.py:480
Async XLA Ops:
  0.6 0.7 %copy-start.1 = (s32[512]{0:T(512)S(1)}, s32[512]{0:T(512)}, u32[]{:S(2)}) copy-start(s32[512]{0:T(512)} %param.10) | copy-start | bytes 6148
  1.3 0.7 %copy-start = (bf16[64,128]{1,0:T(8,128)(2,1)S(1)}, bf16[64,128]{1,0:T(8,128)(2,1)}, u32[]{:S(2)}) copy-start(bf16[64,128]{1,0:T(8,128)(2,1)} %param.9) | copy-start | bytes 49156

commit v6 on v5

--- a/solution.py
+++ b/solution.py
@@ -81,8 +81,8 @@
                  docs_hbm, f_hbm, q_hbm, k_hbm, v_hbm, c_hbm,
                  go_hbm, gq_hbm, gk_hbm, gv_hbm, sum_ref,
                  ids_ref, docs_ref, f_ref, q_ref, k_ref, v_ref, c_ref, zn, pt, zt, cv, bk, o_go, o_gq, o_gk, o_gv,
-                 p_out, p_in, z_out, z_in, ld_in, rd_in, rolled, folded, same, masks, part, got, ring, whole, energy,
-                 small_sem, rim_sem, load_sem, save_sem, halo_s, halo_r,
+                 c_rim, q_rim, p_out, p_in, z_out, z_in, ld_in, rd_in, rolled, folded, same, masks, part, got, ring, whole, energy,
+                 known, small_sem, rim_sem, load_sem, save_sem, halo_s, halo_r,
                  send_a, recv_a, send_b, recv_b, send_c, recv_c, send_d, recv_d):
     me, tp = lax.axis_index("seq"), lax.axis_index("tp")
     blocks, groups, tiles = rows_n // BLK, chans // CH, chans // TILE
@@ -105,24 +105,30 @@
         return pl.ds(pl.multiple_of(i * slab, slab), slab)
 
     barrier = pltpu.get_barrier_semaphore()
-    others = [far(d) for d in range(1, tall)]
-    others += [plane(d, e) for d in range(QUAD) for e in range(wide) if d or e]
-    others += [{"seq": left, "tp": tp}, {"seq": right, "tp": tp}]
-    for to in others:
-        pl.semaphore_signal(barrier, inc=1, device_id=to, device_id_type=MESH)
+    line = wide // 2
+    along = (tp // line) * line
+    others = [{"seq": left, "tp": tp}, {"seq": right, "tp": tp}]
+    others += [near(d) for d in range(1, QUAD)]
+    others += [far(1), far(tall - 1)]
+    others += [{"seq": me, "tp": along + lax.rem(tp + d, line)} for d in (1, line - 1)]
+    others += [{"seq": me, "tp": lax.rem(tp + line, wide)}]
+
+    def greet(sem):
+        for to in others:
+            pl.semaphore_signal(sem, inc=1, device_id=to, device_id_type=MESH)
+
+    greet(barrier)
 
     small = [pltpu.make_async_copy(src, dst, small_sem.at[i]) for i, (src, dst) in enumerate(
         ((docs_hbm, ids_ref), (docs_hbm, docs_ref), (f_hbm, f_ref)))]
     tail, head = pl.ds(rows_n - BLK, BLK), pl.ds(0, BLK)
-    low_rows, high_rows = pl.ds(0, rows_n - BLK), pl.ds(BLK, rows_n - BLK)
-    rims = [pltpu.make_async_copy(src.at[r], dst.at[r], rim_sem.at[i]) for i, (src, dst, r) in enumerate(
-        ((c_hbm, c_ref, head), (q_hbm, q_ref, head), (k_hbm, k_ref, tail), (v_hbm, v_ref, tail)))]
-    start(rims[:2])
+    rims = [pltpu.make_async_copy(src.at[head], dst, rim_sem.at[i]) for i, (src, dst) in enumerate(((c_hbm, c_rim), (q_hbm, q_rim)))]
+    start(rims)
     start(small)
-    start(rims[2:])
-    rest = [pltpu.make_async_copy(src.at[r], dst.at[r], load_sem.at[i]) for i, (src, dst, r) in enumerate(
-        ((k_hbm, k_ref, low_rows), (v_hbm, v_ref, low_rows), (c_hbm, c_ref, high_rows), (q_hbm, q_ref, high_rows)))]
-    start(rest)
+    loads = [[pltpu.make_async_copy(src.at[:, pl.ds(t * TILE, TILE)], dst.at[:, pl.ds(t * TILE, TILE)], load_sem.at[t, i])
+              for i, (src, dst) in enumerate(((k_hbm, k_ref), (v_hbm, v_ref), (c_hbm, c_ref), (q_hbm, q_ref)))] for t in range(tiles)]
+    for t in range(tiles):
+        start(loads[t])
 
     def tile_cols(t):
         return pl.ds(t * TILE, TILE)
@@ -139,7 +145,7 @@
               for d in range(1, QUAD)]
     slot = side * wide + tp
     tell = [remote(energy.at[slot], energy.at[slot], send_d.at[d * wide + e], recv_d.at[d * wide + e], plane(d, e))
-            for d in range(QUAD) for e in range(wide) if d or e]
+            for e in sorted(range(wide), key=lambda e: -min(e % (wide // 2), wide // 2 - e % (wide // 2))) for d in (2, 1, 3, 0) if d or e]
 
     row = lax.broadcasted_iota(jnp.int32, (BLK, BLK), 0)
     lane = lax.broadcasted_iota(jnp.int32, (BLK, BLK), 1)
@@ -151,38 +157,29 @@
     across = [jnp.broadcast_to(d.astype(F32), (BLK, BLK)) for d in docs]
     for b in range(blocks):
         same[b] = jnp.where((lane <= row) & (across[b].T == across[b]), 1.0, 0.0)
-    taps = f_ref[0].astype(F32)
-    for s in range(8):
-        rolled[pl.ds(s, groups, stride=8), :] = pltpu.roll(taps, s, 1) if s else taps
     m_cur = [mask_of(docs[b], first[b]) for b in range(blocks)]
     for b in range(blocks):
         masks[blocks + b] = m_cur[b]
     for b in range(1, blocks):
         masks[b] = mask_of(docs[b - 1], first[b])
 
-    for copy in rims[:2]:
+    for copy in rims:
         copy.wait()
-    z_out[...] = wide_mul(c_ref[head, :], q_ref[head, :])
-    for copy in rims[2:]:
-        copy.wait()
-    p_out[...] = wide_mul(k_ref[tail, :], v_ref[tail, :])
-    for copy in rest:
-        copy.wait()
-
-    def prepare(t, carry):
-        cols = pl.ds(pl.multiple_of(t * TILE, TILE), TILE)
+    z_out[...] = wide_mul(c_rim[...], q_rim[...])
+    for t in range(tiles):
+        for copy in loads[t]:
+            copy.wait()
+        cols = pl.ds(t * TILE, TILE)
         for b in range(blocks):
             r = pl.ds(BLK * b, BLK)
             pt[b + 1, cols, :] = wide_mul(k_ref[r, cols], v_ref[r, cols]).T
             z = wide_mul(c_ref[r, cols], q_ref[r, cols])
             zn[r, cols] = z
             zt[b, cols, :] = z.T
-        return carry
-
-    lax.fori_loop(0, tiles, prepare, 0)
     pl.semaphore_wait(barrier, len(others))
     halo_d.start()
     start(halo_z)
+    greet(known.at[0])
 
     nothing = jnp.zeros((CH, BLK), BF16)
     zero = jnp.concatenate([nothing, nothing], 1)
@@ -224,8 +221,13 @@
                 folded[pl.ds(spot(t, g + i)[1], 8), :] = fold(acc[i])
         return carry
 
-    lax.fori_loop(0, tiles, inner_pairs, 0)
-    start(halo_p)
+    lax.fori_loop(0, tiles // 2, inner_pairs, 0)
+    p_out[...] = wide_mul(k_ref[tail, :], v_ref[tail, :])
+    pl.semaphore_wait(known.at[0], len(others))
+    greet(known.at[1])
+    lax.fori_loop(tiles // 2, tiles, inner_pairs, 0)
+    pl.semaphore_wait(known.at[1], len(others))
+    greet(known.at[2])
 
     halo_d.wait_recv()
     rdocs = jnp.where(me == count - 1, -1, rd_in[...])
@@ -248,6 +250,10 @@
         raw = raw + pltpu.roll(folded[pl.ds(i, groups, stride=8), :], BLK - i, 1)
     part[...] = raw
     start(scatter)
+    start(halo_p)
+    taps = f_ref[0].astype(F32)
+    for s in range(8):
+        rolled[pl.ds(s, groups, stride=8), :] = pltpu.roll(taps, s, 1) if s else taps
 
     d_next = docs[1:] + [rdocs]
     m_last = [mask_of(docs[b], last[b]) for b in range(blocks)]
@@ -324,6 +330,7 @@
     for d in range(1, QUAD):
         mine = mine + got[d]
     ring[up] = mine
+    pl.semaphore_wait(known.at[2], len(others))
     start(climb)
     arrive(halo_p)
     masks[0] = mask_of(jnp.where(me == 0, -1, ld_in[...]), first[0])
@@ -370,11 +377,11 @@
         out_specs=(anywhere,) * 4 + (vm,),
         scratch_shapes=[pltpu.SMEM(docs.shape, jnp.int32), pltpu.VMEM(docs.shape, jnp.int32), pltpu.VMEM(filters.shape, BF16)]
         + [big] * 5 + [pltpu.VMEM((blocks + 1, chans, BLK), BF16)] * 2 + [pltpu.VMEM((blocks, TILE, BLK), BF16)] * 2
-        + [big] * 4 + [rim] * 4 + [line] * 2
+        + [big] * 4 + [rim] * 6 + [line] * 2
         + [pltpu.VMEM((8 * groups, BLK), F32)] * 2 + [pltpu.VMEM((blocks, BLK, BLK), F32), pltpu.VMEM((n_masks, CH, BLK), BF16),
            pltpu.VMEM((groups, BLK), F32), pltpu.VMEM((QUAD, slab, BLK), F32), pltpu.VMEM((tall, slab, BLK), F32),
            pltpu.VMEM((groups, BLK), F32), pltpu.VMEM((QUAD * wide, 1, BLK), F32)]
-        + [dma(3), dma(4), dma(4), dma(tiles, 4), dma(tiles + 3), dma(tiles + 3),
+        + [pltpu.SemaphoreType.REGULAR((3,)), dma(3), dma(2), dma(tiles, 4), dma(tiles, 4), dma(tiles + 3), dma(tiles + 3),
            dma(QUAD), dma(QUAD), dma(tall), dma(tall), dma(QUAD), dma(QUAD), dma(QUAD * wide), dma(QUAD * wide)],
         compiler_params=pltpu.CompilerParams(collective_id=0, has_side_effects=True, vmem_limit_bytes=FUSED_VMEM),
         cost_estimate=pl.CostEstimate(flops=2 * 10**9, bytes_accessed=8 * 2**20, transcendentals=0),

time: 36 us -> 35.8 us (level)
  no operation moved by 1% of the time
where the time goes in v6:
time: 35.8 us; the launch traced here: 35.6 us
  Pallas kernels  33.6 us (94%)
  local copies, waits for them, and re-layouts  1.39 us (4%)
  between operations  0.65 us (2%)
    pallas_call x1, Pallas kernels, fused_call(): pl.pallas_call(functools.partial(fused_kernel, count, wide, bound, chans,...  31.4 us
    pallas_call x1, Pallas kernels, finish_call(): pl.pallas_call(functools.partial(finish_kernel, blocks, chans // TILE), o...  2.2 us
    unnamed x4, local copies, waits for them, and re-layouts  1.39 us

profile of v6, /device:TPU:1, one launch (start us, length us, event | category | flops | bytes accessed | tf_op | source)
XLA Modules:
  0.0 35.6 jit_solution(9672487407550766801)
XLA Ops:
  0.6 0.0 copy-start.1
  0.6 0.7 %copy-done.1 = s32[512]{0:T(512)S(1)} copy-done((s32[512]{0:T(512)S(1)}, s32[512]{0:T(512)}, u32[]{:S(2)}) %copy-start.1) | copy-done | bytes 2072
  1.3 0.0 copy-start
  1.3 0.7 %copy-done = bf16[64,128]{1,0:T(8,128)(2,1)S(1)} copy-done((bf16[64,128]{1,0:T(8,128)(2,1)S(1)}, bf16[64,128]{1,0:T(8,128)(2,1)}, u32[]{:S(2)}) %copy-start) | copy-done | bytes 16408
  2.0 31.4 %fused.1 = (bf16[512,1024]{1,0:T(8,128)(2,1)S(1)}, bf16[512,1024]{1,0:T(8,128)(2,1)S(1)}, bf16[512,1024]{1,0:T(8,128)(2,1)S(1)}, bf16[512,1024]{1,0:T(8,128)(2,1)S(1)}, f32[64,128]{1,0:T(8,128)S(1)}) custom-call(s32[4,128]{1,0:T(4,128)S(1)} %bitcast.4, bf16[1,64,128]{2,1,0:T(8,128)(2,1)S(1)} %bitcast.2, bf16[512,1024]{1,0:T(8,128)(2,1)} %q_hbm.3, ...), custom_call_target="tpu_custom_call" | custom-call | flops 2000000000 | bytes 8388608 | tf_op jit(solution)/shard_map/fused/pallas_call | solution.py:373
  33.4 2.2 %finish.1 = (bf16[512,1024]{1,0:T(8,128)(2,1)}, bf16[512,1024]{1,0:T(8,128)(2,1)}, bf16[512,1024]{1,0:T(8,128)(2,1)}, bf16[512,1024]{1,0:T(8,128)(2,1)}, f32[64,128]{1,0:T(8,128)}) custom-call(s32[4,128]{1,0:T(4,128)S(1)} %bitcast.5, bf16[1,64,128]{2,1,0:T(8,128)(2,1)S(1)} %bitcast.3, f32[64,128]{1,0:T(8,128)S(1)} %get-tuple-element.10.total_hbm, ...), custom_call_target="tpu_custom_call" | custom-call | tf_op jit(solution)/shard_map/finish/pallas_call | solution.py:487
Async XLA Ops:
  0.6 0.7 %copy-start.1 = (s32[512]{0:T(512)S(1)}, s32[512]{0:T(512)}, u32[]{:S(2)}) copy-start(s32[512]{0:T(512)} %param.10) | copy-start | bytes 6148
  1.3 0.7 %copy-start = (bf16[64,128]{1,0:T(8,128)(2,1)S(1)}, bf16[64,128]{1,0:T(8,128)(2,1)}, u32[]{:S(2)}) copy-start(bf16[64,128]{1,0:T(8,128)(2,1)} %param.9) | copy-start | bytes 49156

commit v7 on v6

--- a/solution.py
+++ b/solution.py
@@ -166,6 +166,10 @@
     for copy in rims:
         copy.wait()
     z_out[...] = wide_mul(c_rim[...], q_rim[...])
+    pl.semaphore_wait(barrier, len(others))
+    halo_d.start()
+    start(halo_z)
+    greet(known.at[0])
     for t in range(tiles):
         for copy in loads[t]:
             copy.wait()
@@ -176,10 +180,6 @@
             z = wide_mul(c_ref[r, cols], q_ref[r, cols])
             zn[r, cols] = z
             zt[b, cols, :] = z.T
-    pl.semaphore_wait(barrier, len(others))
-    halo_d.start()
-    start(halo_z)
-    greet(known.at[0])
 
     nothing = jnp.zeros((CH, BLK), BF16)
     zero = jnp.concatenate([nothing, nothing], 1)

time: 35.8 us -> 35.8 us (level)
  no operation moved by 1% of the time
where the time goes in v7:
time: 35.8 us; the launch traced here: 35.6 us
  Pallas kernels  33.5 us (94%)
  local copies, waits for them, and re-layouts  1.39 us (4%)
  between operations  0.65 us (2%)
    pallas_call x1, Pallas kernels, fused_call(): pl.pallas_call(functools.partial(fused_kernel, count, wide, bound, chans,...  31.3 us
    pallas_call x1, Pallas kernels, finish_call(): pl.pallas_call(functools.partial(finish_kernel, blocks, chans // TILE), o...  2.2 us
    unnamed x4, local copies, waits for them, and re-layouts  1.39 us

profile of v7, /device:TPU:1, one launch (start us, length us, event | category | flops | bytes accessed | tf_op | source)
XLA Modules:
  0.0 35.6 jit_solution(4077457923167944009)
XLA Ops:
  0.6 0.0 copy-start.1
  0.6 0.7 %copy-done.1 = s32[512]{0:T(512)S(1)} copy-done((s32[512]{0:T(512)S(1)}, s32[512]{0:T(512)}, u32[]{:S(2)}) %copy-start.1) | copy-done | bytes 2072
  1.3 0.0 copy-start
  1.3 0.7 %copy-done = bf16[64,128]{1,0:T(8,128)(2,1)S(1)} copy-done((bf16[64,128]{1,0:T(8,128)(2,1)S(1)}, bf16[64,128]{1,0:T(8,128)(2,1)}, u32[]{:S(2)}) %copy-start) | copy-done | bytes 16408
  2.0 31.3 %fused.1 = (bf16[512,1024]{1,0:T(8,128)(2,1)S(1)}, bf16[512,1024]{1,0:T(8,128)(2,1)S(1)}, bf16[512,1024]{1,0:T(8,128)(2,1)S(1)}, bf16[512,1024]{1,0:T(8,128)(2,1)S(1)}, f32[64,128]{1,0:T(8,128)S(1)}) custom-call(s32[4,128]{1,0:T(4,128)S(1)} %bitcast.4, bf16[1,64,128]{2,1,0:T(8,128)(2,1)S(1)} %bitcast.2, bf16[512,1024]{1,0:T(8,128)(2,1)} %q_hbm.3, ...), custom_call_target="tpu_custom_call" | custom-call | flops 2000000000 | bytes 8388608 | tf_op jit(solution)/shard_map/fused/pallas_call | solution.py:373
  33.4 2.2 %finish.1 = (bf16[512,1024]{1,0:T(8,128)(2,1)}, bf16[512,1024]{1,0:T(8,128)(2,1)}, bf16[512,1024]{1,0:T(8,128)(2,1)}, bf16[512,1024]{1,0:T(8,128)(2,1)}, f32[64,128]{1,0:T(8,128)}) custom-call(s32[4,128]{1,0:T(4,128)S(1)} %bitcast.5, bf16[1,64,128]{2,1,0:T(8,128)(2,1)S(1)} %bitcast.3, f32[64,128]{1,0:T(8,128)S(1)} %get-tuple-element.10.total_hbm, ...), custom_call_target="tpu_custom_call" | custom-call | tf_op jit(solution)/shard_map/finish/pallas_call | solution.py:487
Async XLA Ops:
  0.6 0.7 %copy-start.1 = (s32[512]{0:T(512)S(1)}, s32[512]{0:T(512)}, u32[]{:S(2)}) copy-start(s32[512]{0:T(512)} %param.10) | copy-start | bytes 6148
  1.3 0.7 %copy-start = (bf16[64,128]{1,0:T(8,128)(2,1)S(1)}, bf16[64,128]{1,0:T(8,128)(2,1)}, u32[]{:S(2)}) copy-start(bf16[64,128]{1,0:T(8,128)(2,1)} %param.9) | copy-start | bytes 49156
